TPU v7x, 32 devices: a whole 2x2x4 slice. The times are simulated.
32 devices in a mesh: grp: 2 (over x), seq: 16 (over z, y, core).
Axes of the slice: x: 2, y: 2, z: 4, core: 2. Of those that a mesh axis runs over, the one named last changes fastest.
Arguments:
- layer_input: bfloat16 [2, 8192, 1024], P('grp', 'seq'), may hold values from -6 to 6
- segment_ids: int32 [2, 8192], P('grp', 'seq'), may hold values from 0 to 15, never falling along the last dimension, each value on 1 to 2048 neighbouring positions
- context_mask: int32 [2, 16, 128], P('grp', 'seq'), may hold values 0 or 1
- first_gain: float32 [1024], replicated, may hold values from 0.5 to 1.5
- attention_in: bfloat16 [1024, 3072], replicated, may hold values from -0.1875 to 0.1875
- kernel_weight: float32 [1024, 16], replicated, may hold values from -1.5 to 1.5
- kernel_decay: float32 [1024, 16], replicated, may hold values from -1 to 7
- attention_out: bfloat16 [1024, 1024], replicated, may hold values from -0.75 to 0.75
- second_gain: float32 [1024], replicated, may hold values from 0.5 to 1.5
- expand_weight: bfloat16 [1024, 4096], replicated, may hold values from -0.1875 to 0.1875
- reduce_weight: bfloat16 [4096, 1024], replicated, may hold values from -0.09375 to 0.09375
- cotangent: bfloat16 [2, 8192, 1024], P('grp', 'seq'), may hold values from -6 to 6
Outputs:
- layer_output: bfloat16 [2, 8192, 1024], P('grp', 'seq')
- input_grad: float32 [2, 8192, 1024], P('grp', 'seq')
- first_gain_grad: float32 [1024], P('seq')
- attention_in_grad: float32 [1024, 3072], P('seq')
- kernel_weight_grad: float32 [1024, 16], P('seq')
- kernel_decay_grad: float32 [1024, 16], P('seq')
- attention_out_grad: float32 [1024, 1024], P('seq')
- second_gain_grad: float32 [1024], P('seq')
- expand_weight_grad: float32 [1024, 4096], P('seq')
- reduce_weight_grad: float32 [4096, 1024], P('seq')
Inputs may be any that keep to these rules, and one draw needn't show every extreme that they name: `segment_ids`: within a sequence segment numbers never fall; each document has 1 to 2048 positions, and one has exactly that many.
All inputs are finite; a program needn't handle non-finite values. No bound on the sum of `context_mask` on one device may be relied on, other than what follows from the above.
Results may differ from a plain program's by a relative error of at most 0.015.
Values may be sent and summed in bfloat16 or wider, within the bound.
A program may use at most 256 MiB of HBM per device.

v0:
```python
import math

import jax
import jax.numpy as jnp
from jax import lax
from jax.sharding import PartitionSpec as P

HEADS = 8
HEAD_DIM = 128
BLK = 512
CTX = 128


epsilon = 1e-05
highest = lax.Precision.HIGHEST
triple = lax.Precision.HIGH
masked_score = -1e30


def shifted(value, axis, steps):
    count = lax.axis_size(axis)
    first, last = (max(0, -steps), min(count, count - steps))
    return lax.ppermute(value, axis, [(source, source + steps) for source in range(first, last)])


def layer_norm(matrix, scales):
    centre = matrix - jnp.mean(matrix, axis=-1, keepdims=True)
    spread = jnp.mean(centre * centre, axis=-1, keepdims=True)
    return centre * lax.rsqrt(spread + epsilon) * scales


def activation(values_in):
    return jax.nn.gelu(values_in, approximate=True)


def low_product(operand, partner):
    return jnp.dot(operand, partner, preferred_element_type=jnp.float32)


def inner_rows(operand, partner):
    return lax.dot_general(
        operand, partner, (((0,), (0,)), ((), ())), preferred_element_type=jnp.float32
    )


def against_rows(operand, partner):
    return lax.dot_general(
        operand, partner, (((1,), (1,)), ((), ())), preferred_element_type=jnp.float32
    )


def exact_left(table, stacked):
    return jnp.einsum(
        "kn,cnm->ckm", table, stacked, precision=highest, preferred_element_type=jnp.float32
    )


def split_left(table, stacked):
    upper = table.astype(jnp.bfloat16)
    lower = (table - upper.astype(jnp.float32)).astype(jnp.bfloat16)
    first_term = jnp.einsum("kn,cnm->ckm", upper, stacked, preferred_element_type=jnp.float32)
    second_term = jnp.einsum("kn,cnm->ckm", lower, stacked, preferred_element_type=jnp.float32)
    return first_term + second_term


def close_left(table, stacked):
    return jnp.einsum(
        "kn,cnm->ckm", table, stacked, precision=triple, preferred_element_type=jnp.float32
    )


def close_right(stacked, table):
    return jnp.einsum(
        "ckn,nm->ckm", stacked, table, precision=triple, preferred_element_type=jnp.float32
    )


def angle_tables(length):
    counter = jnp.arange(length, dtype=jnp.int32)
    phases = counter[:, None] * counter[None, :] % length
    angles = phases.astype(jnp.float32) * (2.0 * math.pi / length)
    return (jnp.cos(angles), jnp.sin(angles))


def turn_tables(first_rows, second_rows):
    first_count = jnp.arange(first_rows, dtype=jnp.int32)
    second_count = jnp.arange(second_rows, dtype=jnp.int32)
    angles = (first_count[:, None] * second_count[None, :]).astype(jnp.float32) * (
        2.0 * math.pi / (first_rows * second_rows)
    )
    return (jnp.cos(angles), jnp.sin(angles))


def factor_sizes(length):
    padded_total = 2 * length
    bit_count = padded_total.bit_length() - 1
    first_rows = math.gcd(padded_total, 1 << bit_count // 2)
    return (first_rows, padded_total // first_rows)


def forward_transform(signal):
    channels, length = signal.shape
    first_rows, second_rows = factor_sizes(length)
    cosine_first, sine_first = angle_tables(first_rows)
    cosine_second, sine_second = angle_tables(second_rows)
    turn_cosine, turn_sine = turn_tables(first_rows, second_rows)
    halves = first_rows // 2
    stacked = signal.reshape(channels, halves, second_rows)
    if signal.dtype == jnp.bfloat16:
        real_part = split_left(cosine_first[:, :halves], stacked)
        imag_part = -split_left(sine_first[:, :halves], stacked)
    else:
        real_part = exact_left(cosine_first[:, :halves], stacked)
        imag_part = -exact_left(sine_first[:, :halves], stacked)
    turned_real = real_part * turn_cosine + imag_part * turn_sine
    turned_imag = imag_part * turn_cosine - real_part * turn_sine
    spectrum_real = close_right(turned_real, cosine_second) + close_right(turned_imag, sine_second)
    spectrum_imag = close_right(turned_imag, cosine_second) - close_right(turned_real, sine_second)
    return (spectrum_real, spectrum_imag)


def inverse_transform(spectrum_real, spectrum_imag, length):
    channels = spectrum_real.shape[0]
    first_rows, second_rows = factor_sizes(length)
    cosine_first, sine_first = angle_tables(first_rows)
    cosine_second, sine_second = angle_tables(second_rows)
    turn_cosine, turn_sine = turn_tables(first_rows, second_rows)
    halves = first_rows // 2
    mixed_real = close_right(spectrum_real, cosine_second) - close_right(spectrum_imag, sine_second)
    mixed_imag = close_right(spectrum_real, sine_second) + close_right(spectrum_imag, cosine_second)
    turned_real = mixed_real * turn_cosine - mixed_imag * turn_sine
    turned_imag = mixed_real * turn_sine + mixed_imag * turn_cosine
    signal = close_left(cosine_first[:halves], turned_real) - close_left(
        sine_first[:halves], turned_imag
    )
    return signal.reshape(channels, length) / (2.0 * length)


def lag_kernel(weights, decays, length):
    decay_rates = jnp.exp(decays) / length
    lag_steps = jnp.arange(length, dtype=jnp.float32)
    return jnp.einsum(
        "cn,cnl->cl",
        weights * jnp.sqrt(decay_rates),
        jnp.exp(-decay_rates[:, :, None] * lag_steps),
        precision=highest,
    )


def local(
    layer_input,
    segment_ids,
    context_mask,
    first_gain,
    attention_in,
    kernel_weight,
    kernel_decay,
    attention_out,
    second_gain,
    expand_weight,
    reduce_weight,
    cotangent,
):
    seq_count = lax.axis_size("seq")
    device_place = lax.axis_index("seq")
    tokens = layer_input.shape[1]
    model_width = layer_input.shape[2]
    blocks = tokens // BLK
    length_all = tokens * seq_count
    channels = model_width // seq_count
    offsets = jnp.arange(BLK)
    inputs = layer_input[0].astype(jnp.float32)
    normed_one, norm_one_back = jax.vjp(layer_norm, inputs, first_gain)
    first_low = normed_one.astype(jnp.bfloat16)
    packed = low_product(first_low, attention_in).astype(jnp.bfloat16)
    lag_weights = lax.dynamic_slice_in_dim(kernel_weight, device_place * channels, channels, 0)
    lag_decays = lax.dynamic_slice_in_dim(kernel_decay, device_place * channels, channels, 0)

    def kernel_local(weights, decays):
        return lag_kernel(weights, decays, length_all)

    kernel, kernel_back = jax.vjp(kernel_local, lag_weights, lag_decays)
    signal = lax.all_to_all(first_low.T, "seq", split_axis=0, concat_axis=1, tiled=True)
    signal_real, signal_imag = forward_transform(signal)
    kernel_real, kernel_imag = forward_transform(kernel)
    convolved = inverse_transform(
        signal_real * kernel_real - signal_imag * kernel_imag,
        signal_real * kernel_imag + signal_imag * kernel_real,
        length_all,
    )
    tail_rows = convolved.reshape(channels, seq_count * blocks, BLK)[:, :, BLK - CTX :].astype(
        jnp.bfloat16
    )
    states = lax.all_to_all(
        tail_rows.reshape(channels, seq_count * blocks * CTX),
        "seq",
        split_axis=1,
        concat_axis=0,
        tiled=True,
    ).T
    groups = states.reshape(blocks, CTX, model_width)
    earlier = shifted(groups[blocks - 1], "seq", 1)
    context = jnp.concatenate([earlier[None], groups[: blocks - 1]], axis=0).reshape(
        blocks * CTX, model_width
    )
    pair_weight = attention_in[:, model_width:]
    context_pairs = low_product(context, pair_weight).astype(jnp.bfloat16)

    def block_parts(block_index):
        first_row = block_index * BLK
        segments = segment_ids[0, first_row : first_row + BLK]
        inside = (offsets[None, :] <= offsets[:, None]) & (segments[None, :] == segments[:, None])
        visible = (context_mask[0, block_index] == 1) & (device_place * blocks + block_index > 0)
        allowed = jnp.concatenate([inside, jnp.broadcast_to(visible[None, :], (BLK, CTX))], axis=1)
        queries = packed[first_row : first_row + BLK, :model_width].reshape(BLK, HEADS, HEAD_DIM)
        block_pairs = packed[first_row : first_row + BLK, model_width:]
        joined = jnp.concatenate([block_pairs, context_pairs], axis=0)
        keys_all = joined[:, :model_width].reshape(BLK + CTX, HEADS, HEAD_DIM)
        values_all = joined[:, model_width:].reshape(BLK + CTX, HEADS, HEAD_DIM)
        return (allowed, queries, keys_all, values_all)

    def masked_scores(allowed, queries, keys_all):
        raw_scores = jnp.einsum(
            "qhd,khd->hqk", queries, keys_all, preferred_element_type=jnp.float32
        ) / math.sqrt(HEAD_DIM)
        return jnp.where(allowed[None], raw_scores, masked_score)

    block_index = 0
    allowed, queries, keys_all, values_all = block_parts(block_index)
    scores = masked_scores(allowed, queries, keys_all)
    row_top = jnp.max(scores, axis=-1, keepdims=True)
    exponent = jnp.exp(scores - row_top)
    row_total = jnp.sum(exponent, axis=-1, keepdims=True)
    probabilities = (exponent / row_total).astype(jnp.bfloat16)
    mixture = jnp.einsum(
        "hqk,khd->qhd", probabilities, values_all, preferred_element_type=jnp.float32
    )
    attended_parts = mixture.reshape(BLK, model_width)
    log_totals = [row_top + jnp.log(row_total)]
    attended = attended_parts.astype(jnp.bfloat16)
    residual = inputs + low_product(attended, attention_out)
    normed_two, norm_two_back = jax.vjp(layer_norm, residual, second_gain)
    second_low = normed_two.astype(jnp.bfloat16)
    expanded = low_product(second_low, expand_weight)
    activated_full, gelu_back = jax.vjp(activation, expanded)
    activated = activated_full.astype(jnp.bfloat16)
    output = (residual + low_product(activated, reduce_weight)).astype(jnp.bfloat16)
    upstream = cotangent[0]
    reduce_grad = inner_rows(activated, upstream)
    activated_grad = against_rows(upstream, reduce_weight)
    expanded_grad = gelu_back(activated_grad)[0].astype(jnp.bfloat16)
    expand_grad = inner_rows(second_low, expanded_grad)
    residual_part, second_gain_grad = norm_two_back(against_rows(expanded_grad, expand_weight))
    residual_grad = upstream.astype(jnp.float32) + residual_part
    branch_grad = residual_grad.astype(jnp.bfloat16)
    out_grad = inner_rows(attended, branch_grad)
    attended_grad = against_rows(branch_grad, attention_out).astype(jnp.bfloat16)
    block_index = 0
    allowed, queries, keys_all, values_all = block_parts(block_index)
    scores = masked_scores(allowed, queries, keys_all)
    probs_full = jnp.exp(scores - log_totals[block_index])
    probabilities = probs_full.astype(jnp.bfloat16)
    mixture_grad = attended_grad.reshape(BLK, HEADS, HEAD_DIM)
    values_grad = jnp.einsum(
        "hqk,qhd->khd", probabilities, mixture_grad, preferred_element_type=jnp.float32
    )
    weights_grad = jnp.einsum(
        "qhd,khd->hqk", mixture_grad, values_all, preferred_element_type=jnp.float32
    )
    row_dot = jnp.sum(probs_full * weights_grad, axis=-1, keepdims=True)
    scores_grad = (probs_full * (weights_grad - row_dot)).astype(jnp.bfloat16)
    queries_grad = jnp.einsum(
        "hqk,khd->qhd", scores_grad, keys_all, preferred_element_type=jnp.float32
    ) / math.sqrt(HEAD_DIM)
    keys_grad = jnp.einsum(
        "hqk,qhd->khd", scores_grad, queries, preferred_element_type=jnp.float32
    ) / math.sqrt(HEAD_DIM)
    keys_flat = keys_grad.reshape(BLK + CTX, model_width)
    values_flat = values_grad.reshape(BLK + CTX, model_width)
    packed_grads = jnp.concatenate(
        [queries_grad.reshape(BLK, model_width), keys_flat[:BLK], values_flat[:BLK]], axis=1
    )
    context_grads = jnp.concatenate([keys_flat[BLK:], values_flat[BLK:]], axis=1)
    packed_grad = packed_grads.astype(jnp.bfloat16)
    context_pairs_grad = context_grads.astype(jnp.bfloat16)
    pair_grad = inner_rows(context, context_pairs_grad)
    qkv_grad = inner_rows(first_low, packed_grad) + jnp.concatenate(
        [jnp.zeros((model_width, model_width), jnp.float32), pair_grad], axis=1
    )
    context_grad = against_rows(context_pairs_grad, pair_weight).astype(jnp.bfloat16)
    group_grads = context_grad.reshape(blocks, CTX, model_width)
    later = shifted(group_grads[0], "seq", -1)
    tail_grads = jnp.concatenate([group_grads[1:], later[None]], axis=0).reshape(
        blocks * CTX, model_width
    )
    tail_channels = lax.all_to_all(tail_grads.T, "seq", split_axis=0, concat_axis=1, tiled=True)
    field_grad = jnp.concatenate(
        [
            jnp.zeros((channels, seq_count * blocks, BLK - CTX), jnp.bfloat16),
            tail_channels.reshape(channels, seq_count * blocks, CTX),
        ],
        axis=2,
    ).reshape(channels, length_all)
    held_signal = (signal_real, signal_imag)
    held_kernel = (kernel_real, kernel_imag)
    grad_real, grad_imag = forward_transform(field_grad)
    signal_grad = inverse_transform(
        held_kernel[0] * grad_real + held_kernel[1] * grad_imag,
        held_kernel[0] * grad_imag - held_kernel[1] * grad_real,
        length_all,
    )
    kernel_grad = inverse_transform(
        held_signal[0] * grad_real + held_signal[1] * grad_imag,
        held_signal[0] * grad_imag - held_signal[1] * grad_real,
        length_all,
    )
    weight_shard_grad, decay_shard_grad = kernel_back(kernel_grad)
    signal_tokens = lax.all_to_all(
        signal_grad.astype(jnp.bfloat16), "seq", split_axis=1, concat_axis=0, tiled=True
    ).T.astype(jnp.float32)
    normed_one_grad = against_rows(packed_grad, attention_in) + signal_tokens
    input_part, first_gain_grad = norm_one_back(normed_one_grad)
    input_grad = residual_grad + input_part
    shares = (
        lax.psum_scatter(first_gain_grad, "seq", scatter_dimension=0, tiled=True),
        lax.psum_scatter(qkv_grad, "seq", scatter_dimension=0, tiled=True),
        lax.psum_scatter(out_grad, "seq", scatter_dimension=0, tiled=True),
        lax.psum_scatter(second_gain_grad, "seq", scatter_dimension=0, tiled=True),
        lax.psum_scatter(expand_grad, "seq", scatter_dimension=0, tiled=True),
        lax.psum_scatter(reduce_grad, "seq", scatter_dimension=0, tiled=True),
    )
    summed = (
        lax.psum(shares[0].astype(jnp.bfloat16), "grp").astype(jnp.float32),
        lax.psum(shares[1].astype(jnp.bfloat16), "grp").astype(jnp.float32),
        lax.psum(shares[2].astype(jnp.bfloat16), "grp").astype(jnp.float32),
        lax.psum(shares[3].astype(jnp.bfloat16), "grp").astype(jnp.float32),
        lax.psum(shares[4].astype(jnp.bfloat16), "grp").astype(jnp.float32),
        lax.psum(shares[5].astype(jnp.bfloat16), "grp").astype(jnp.float32),
        lax.psum(weight_shard_grad.astype(jnp.bfloat16), "grp").astype(jnp.float32),
        lax.psum(decay_shard_grad.astype(jnp.bfloat16), "grp").astype(jnp.float32),
    )
    return (
        output[None],
        input_grad[None],
        summed[0],
        summed[1],
        summed[6],
        summed[7],
        summed[2],
        summed[3],
        summed[4],
        summed[5],
    )


def solution(mesh):
    in_specs = (
        P("grp", "seq", None),
        P("grp", "seq"),
        P("grp", "seq", None),
        P(),
        P(),
        P(),
        P(),
        P(),
        P(),
        P(),
        P(),
        P("grp", "seq", None),
    )
    out_specs = (
        P("grp", "seq", None),
        P("grp", "seq", None),
        P("seq"),
        P("seq", None),
        P("seq", None),
        P("seq", None),
        P("seq", None),
        P("seq"),
        P("seq", None),
        P("seq", None),
    )
    return jax.shard_map(local, mesh=mesh, in_specs=in_specs, out_specs=out_specs, check_vma=False)
```

profile of v0, /device:TPU:0, one launch (start us, length us, event | category | flops | bytes accessed | tf_op | source)
XLA Modules:
  0.0 877.9 jit_solution(7854961165336530806)
XLA Ops:
  13.4 7.4 all-to-all-start
  22.7 21.7 %fusion.1 = f32[64,1,8192]{2,1,0:T(1,128)S(1)} fusion(f32[64,16,1]{1,2,0:T(1,128)S(1)} %bitcast.386, f32[64,16]{1,0:T(8,128)S(1)} %get-tuple-element.48), kind=kOutput, calls=%fused_computation.3 | convolution fusion | flops 109051904 | bytes 2105344 | tf_op jit(solution)/shard_map/jvp(cn,cnl->cl)/dot_general | solution.py:142
  46.0 6.7 fusion.175
  52.7 7.1 fusion.177
  59.8 3.9 fusion.130
  63.7 4.0 fusion.134
  67.7 6.9 convolution_subtract_fusion.4
  74.6 5.6 convolution_add_fusion.4
  86.5 3.7 fusion.109
  90.2 5.4 fusion.105
  95.6 5.4 convolution_add_fusion.5
  101.0 11.0 %multiply_add_fusion.2 = (f32[64,128,128]{2,1,0:T(8,128)}, f32[64,128,128]{2,1,0:T(8,128)}, f32[64,128,128]{2,1,0:T(8,128)}) fusion(f32[64,128,128]{2,1,0:T(8,128)} %convolution_add_fusion.4, f32[64,128,128]{2,1,0:T(8,128)} %convolution_add_fusion.5, f32[64,128,128]{2,1,0:T(8,128)} %convolution_subtract_fusion.4, f32[64,128,128]{2,1,0:T(8,128)} %fusion.105, ...), kind=kOutput, calls=%fused_computation.76 | convolution fusion | flops 816021504 | bytes 37879808 | tf_op jit(solution)/shard_map/ckn,nm->ckm/dot_general | solution.py:73
  112.0 4.4 fusion.164
  125.3 3.7 fusion.92
  133.2 6.1 all-to-all-start.1
  139.4 7.8 convolution_convert_fusion
  156.7 3.0 fusion.57
  164.1 4.2 fusion.331
  172.4 3.8 fusion.83
  177.9 10.8 %fusion.326 = f32[512,4096]{1,0:T(8,128)} fusion(bf16[1024,4096]{1,0:T(8,128)(2,1)} %param.21, f32[512,1024]{1,0:T(8,128)S(1)} %get-tuple-element.54, f32[1024]{0:T(1024)S(1)} %copy-done.53, f32[512]{0:T(512)S(1)} %fusion.219, f32[512]{0:T(512)S(1)} %broadcast_multiply_fusion), kind=kOutput, calls=%fused_computation.368 | convolution fusion | flops 4297064448 | bytes 18882560 | tf_op jit(solution)/shard_map/dot_general | solution.py:37
  188.7 11.8 %fusion.11 = bf16[512,4096]{1,0:T(8,128)(2,1)S(1)} fusion(f32[512,4096]{1,0:T(8,128)} %fusion.326, bf16[4096,1024]{1,0:T(8,128)(2,1)S(1)} %bitcast.389, bf16[1,512,1024]{2,1,0:T(8,128)(2,1)S(1)} %copy-done.25), kind=kOutput, calls=%fused_computation.22 | convolution fusion | flops 4336910336 | bytes 22020096 | tf_op jit(solution)/shard_map/dot_general | solution.py:47
  200.6 9.5 %multiply_reduce_fusion.2 = (f32[1024]{0:T(1024)}, f32[512]{0:T(512)S(1)}, f32[512,1024]{1,0:T(8,128)S(1)}) fusion(f32[512,1024]{1,0:T(8,128)S(1)} %get-tuple-element.54, f32[512]{0:T(512)S(1)} %fusion.219, f32[512]{0:T(512)S(1)} %broadcast_multiply_fusion, f32[1024]{0:T(1024)S(1)} %copy-done.53, bf16[512,4096]{1,0:T(8,128)(2,1)S(1)} %fusion.11, ...), kind=kOutput, calls=%fused_computation.121 | convolution fusion | flops 4298635776 | bytes 16791552 | tf_op jit(solution)/shard_map/dot_general | solution.py:47
  213.5 3.2 fusion.333
  216.8 3.5 convolution_convert_fusion.1
  222.2 7.2 multiply_reduce_fusion.1
  242.1 9.9 %pad_add_fusion = f32[1024,3072]{1,0:T(8,128)} fusion(f32[1024,2048]{1,0:T(8,128)S(1)} %fusion.136, bf16[512,1024]{0,1:T(8,128)(2,1)S(1)} %bitcast.376, bf16[512,1024]{0,1:T(8,128)(2,1)S(1)} %bitcast.374, bf16[512,1024]{0,1:T(8,128)(2,1)S(1)} %bitcast.382, bf16[1,512,1024]{2,1,0:T(8,128)(2,1)S(1)} %copy-done.11, f32[1024]{0:T(1024)S(1)} %copy-done.40, ...), kind=kOutput, calls=%fused_computation.6 | convolution fusion | flops 3236429824 | bytes 25174016 | tf_op jit(solution)/shard_map/dot_general | solution.py:41
  253.6 10.8 %fusion.325 = f32[1024,4096]{1,0:T(8,128)} fusion(bf16[512,4096]{1,0:T(8,128)(2,1)} %copy-done.56, f32[512,1024]{1,0:T(8,128)S(1)} %copy-done.18, f32[1024]{0:T(1024)S(1)} %copy-done.53, f32[512]{0:T(512)S(1)} %fusion.219, f32[512]{0:T(512)S(1)} %broadcast_multiply_fusion), kind=kOutput, calls=%fused_computation.367 | convolution fusion | flops 4297064448 | bytes 23076864 | tf_op jit(solution)/shard_map/dot_general | solution.py:41
  264.5 15.2 %fusion.123 = f32[4096,1024]{1,0:T(8,128)} fusion(bf16[1,512,1024]{2,1,0:T(8,128)(2,1)} %param.23, f32[512,4096]{1,0:T(8,128)} %fusion.326), kind=kOutput, calls=%fused_computation.168 | convolution fusion | flops 4313841664 | bytes 26214400 | tf_op jit(solution)/shard_map/dot_general | solution.py:41
  279.7 4.5 fusion.118
  288.7 9.8 %all-to-all-start.2 = ((bf16[16,64,128]{2,1,0:T(8,128)(2,1)}), bf16[16,64,128]{2,1,0:T(8,128)(2,1)S(1)}, u32[]{:S(2)}, u32[]{:S(2)}) async-start(bf16[16,64,128]{2,1,0:T(8,128)(2,1)} %bitcast.379), calls=%async_computation.2 | async-start | bytes 524288 | tf_op jit(solution)/shard_map/all_to_all | solution.py:296
  298.6 13.9 %fusion.98 = bf16[1,512,1024]{2,1,0:T(8,128)(2,1)} fusion(f32[512,1024]{1,0:T(8,128)S(1)} %copy-done.18, bf16[4096,1024]{1,0:T(8,128)(2,1)} %param.22, f32[512,4096]{1,0:T(8,128)} %fusion.326), kind=kOutput, calls=%fused_computation.151 | convolution fusion | flops 4314890240 | bytes 19922944 | tf_op jit(solution)/shard_map/dot_general | solution.py:37
  316.8 5.9 fusion.115
  322.8 3.9 fusion.111
  326.7 5.6 convolution_subtract_fusion.2
  332.3 19.7 %multiply_subtract_fusion = (f32[64,128,128]{2,1,0:T(8,128)}, f32[64,128,128]{2,1,0:T(8,128)}, f32[64,128,128]{2,1,0:T(8,128)}, f32[64,128,128]{2,1,0:T(8,128)}) fusion(f32[64,128,128]{2,1,0:T(8,128)} %get-tuple-element.50, f32[64,128,128]{2,1,0:T(8,128)} %convolution_add_fusion.5, f32[64,128,128]{2,1,0:T(8,128)} %convolution_subtract_fusion.2, ...), kind=kOutput, calls=%fused_computation.55 | convolution fusion | flops 822312960 | bytes 50462720 | tf_op jit(solution)/shard_map/ckn,nm->ckm/dot_general | solution.py:73
  352.0 4.4 fusion.159
  365.3 2.9 fusion.95
  369.7 2.8 copy.312
  372.5 6.1 all-to-all-start.3
  378.6 4.6 fusion.156
  397.3 43.3 %fusion = f32[64,1,16]{2,1,0:T(1,128)S(1)} fusion(f32[64,8192,1]{1,2,0:T(1,128)} %bitcast.364, f32[64,16]{1,0:T(8,128)S(1)} %copy-done.42), kind=kOutput, calls=%fused_computation.2 | convolution fusion | flops 109051904 | bytes 2105344 | tf_op jit(solution)/shard_map/transpose(jvp(cn,cnl->cl))/dot_general | solution.py:142
  440.7 9.2 %multiply_reduce_fusion = f32[64,16]{1,0:T(8,128)S(1)} fusion(f32[64,8192]{1,0:T(8,128)S(1)} %bitcast.369, f32[64,16]{1,0:T(8,128)S(1)} %copy-done.44, f32[64,16]{1,0:T(8,128)S(1)} %copy-done.42), kind=kLoop, calls=%fused_computation | loop fusion | flops 41942016 | bytes 2109440 | tf_op jit(solution)/shard_map/transpose(jvp())/reduce_sum | solution.py:145
  457.2 163.6 %reduce-scatter.9.cloned.1.call-done = f32[64,4096]{1,0:T(8,128)} async-done(((f32[1024,4096]{1,0:T(8,128)}), f32[64,4096]{1,0:T(8,128)}) %reduce-scatter.9.cloned.1.call-update) | async-done | bytes 1048592 | tf_op jit(solution)/shard_map/reduce_scatter | solution.py:329
  622.9 180.0 %reduce-scatter.11.cloned.1.call-done = f32[256,1024]{1,0:T(8,128)} async-done(((f32[4096,1024]{1,0:T(8,128)}), f32[256,1024]{1,0:T(8,128)}) %reduce-scatter.11.cloned.1.call-update) | async-done | bytes 1048592 | tf_op jit(solution)/shard_map/reduce_scatter | solution.py:330
  805.1 8.1 fusion.65
  815.6 32.0 %all-reduce.4 = (bf16[1024]{0:T(1024)(128)(2,1)S(1)}, bf16[1024]{0:T(1024)(128)(2,1)S(1)}) all-reduce(f32[1024]{0:T(1024)S(1)} %get-tuple-element.22, f32[1024]{0:T(1024)S(1)} %copy-done.52), channel_id=2, replica_groups=mesh['grp'=2,'seq'=16] {'seq'}, use_global_device_ids=true, to_apply=%region_12.13.clone | all-reduce | flops 2048 | bytes 12288
  847.8 9.2 %all-reduce.5 = (bf16[64,16]{1,0:T(8,128)(2,1)S(1)}, bf16[64,16]{1,0:T(8,128)(2,1)S(1)}, bf16[64]{0:T(256)(128)(2,1)S(1)}, bf16[64]{0:T(256)(128)(2,1)S(1)}) all-reduce(bf16[64,16]{1,0:T(8,128)(2,1)S(1)} %get-tuple-element.47, bf16[64,16]{1,0:T(8,128)(2,1)S(1)} %get-tuple-element.46, ...), channel_id=1, replica_groups=mesh['grp'=2,'seq'=16] {'grp'}, use_global_device_ids=true, to_apply=%region_16.17 | all-reduce | flops 2176 | bytes 8704 | tf_op jit(solution)/shard_map/psum | solution.py:339
  859.4 4.9 add_bitcast_fusion
  (245 shorter events, 123.9 us)
Async XLA Ops:
  7.2 168.9 %copy-start = (bf16[1024,1024]{1,0:T(8,128)(2,1)S(1)}, bf16[1024,1024]{1,0:T(8,128)(2,1)}, u32[]{:S(2)}) copy-start(bf16[1024,1024]{1,0:T(8,128)(2,1)} %param.19) | copy-start | bytes 6291460
  10.4 33.9 %copy-start.49 = (f32[512]{0:T(512)}, f32[512]{0:T(512)S(1)}, u32[]{:S(2)}) copy-start(f32[512]{0:T(512)S(1)} %fusion.64) | copy-start | bytes 6148
  10.4 230.7 %copy-start.45 = (f32[512]{0:T(512)}, f32[512]{0:T(512)S(1)}, u32[]{:S(2)}) copy-start(f32[512]{0:T(512)S(1)} %fusion.218) | copy-start | bytes 6148
  13.4 66.7 %all-to-all-start = ((bf16[16,64,512]{2,1,0:T(8,128)(2,1)}), bf16[16,64,512]{2,1,0:T(8,128)(2,1)S(1)}, u32[]{:S(2)}, u32[]{:S(2)}) async-start(bf16[16,64,512]{2,1,0:T(8,128)(2,1)} %bitcast.368), calls=%async_computation | async-start | bytes 2097152 | tf_op jit(solution)/shard_map/all_to_all | solution.py:183
  21.1 101.7 %copy-start.28 = (f32[128,128]{0,1:T(8,128)}, f32[128,128]{0,1:T(8,128)S(1)}, u32[]{:S(2)}) copy-start(f32[128,128]{0,1:T(8,128)S(1)} %fusion.179) | copy-start | bytes 196612
  21.3 104.0 %copy-start.26 = (f32[128,128]{0,1:T(8,128)}, f32[128,128]{0,1:T(8,128)S(1)}, u32[]{:S(2)}) copy-start(f32[128,128]{0,1:T(8,128)S(1)} %fusion.180) | copy-start | bytes 196612
  21.6 103.7 %copy-start.12 = (f32[128,128]{0,1:T(8,128)}, f32[128,128]{0,1:T(8,128)S(1)}, u32[]{:S(2)}) copy-start(f32[128,128]{0,1:T(8,128)S(1)} %get-tuple-element.62) | copy-start | bytes 196612
  21.6 103.7 %copy-start.14 = (f32[128,128]{0,1:T(8,128)}, f32[128,128]{0,1:T(8,128)S(1)}, u32[]{:S(2)}) copy-start(f32[128,128]{0,1:T(8,128)S(1)} %get-tuple-element.63) | copy-start | bytes 196612
  22.5 21.8 %copy-start.35 = (f32[64,16]{1,0:T(8,128)}, f32[64,16]{1,0:T(8,128)S(1)}, u32[]{:S(2)}) copy-start(f32[64,16]{1,0:T(8,128)S(1)} %copy.422) | copy-start | bytes 12292
  22.6 21.8 %copy-start.37 = (f32[64,16]{1,0:T(8,128)}, f32[64,16]{1,0:T(8,128)S(1)}, u32[]{:S(2)}) copy-start(f32[64,16]{1,0:T(8,128)S(1)} %copy.423) | copy-start | bytes 12292
  22.7 21.7 %copy-start.41 = (f32[64,16]{1,0:T(8,128)}, f32[64,16]{1,0:T(8,128)S(1)}, u32[]{:S(2)}) copy-start(f32[64,16]{1,0:T(8,128)S(1)} %get-tuple-element.48) | copy-start | bytes 12292
  22.7 21.7 %copy-start.43 = (f32[64,16]{1,0:T(8,128)}, f32[64,16]{1,0:T(8,128)S(1)}, u32[]{:S(2)}) copy-start(f32[64,16]{1,0:T(8,128)S(1)} %get-tuple-element.49) | copy-start | bytes 12292
  125.3 14.1 %copy-start.11 = (bf16[1,512,1024]{2,1,0:T(8,128)(2,1)S(1)}, bf16[1,512,1024]{2,1,0:T(8,128)(2,1)}, u32[]{:S(2)}) copy-start(bf16[1,512,1024]{2,1,0:T(8,128)(2,1)} %param.12) | copy-start | bytes 3145732
  125.3 14.1 %copy-start.40 = (f32[1024]{0:T(1024)S(1)}, f32[1024]{0:T(1024)}, u32[]{:S(2)}) copy-start(f32[1024]{0:T(1024)} %param.15) | copy-start | bytes 12292
  133.2 16.2 %all-to-all-start.1 = ((bf16[64,16,128]{2,0,1:T(8,128)(2,1)}), bf16[64,16,128]{2,0,1:T(8,128)(2,1)}, u32[]{:S(2)}, u32[]{:S(2)}) async-start(bf16[64,16,128]{2,0,1:T(8,128)(2,1)} %copy.424), calls=%async_computation.1 | async-start | bytes 524288 | tf_op jit(solution)/shard_map/all_to_all | solution.py:194
  139.3 7.9 copy-start.51
  139.3 12.8 %copy-start.54 = (s32[1,1,128]{2,1,0:T(1,128)S(1)}, s32[1,1,128]{2,1,0:T(1,128)}, u32[]{:S(2)}) copy-start(s32[1,1,128]{2,1,0:T(1,128)} %param.14) | copy-start | bytes 1540
  139.3 314.2 %reduce-scatter.7.cloned.1.call-start = ((), (), s32[]{:S(2)}) async-start(), calls=%async_computation.9 | async-start | bytes 4456448 | tf_op jit(solution)/shard_map/reduce_scatter | solution.py:327
  149.4 7.3 collective-permute-start
  176.1 12.6 %slice-start.4 = ((s8[8388608]{0:T(1024)(128)(4,1)}), s8[4194304]{0:T(1024)(128)(4,1)S(1)}, s32[]{:S(2)}) async-start(s8[8388608]{0:T(1024)(128)(4,1)} %bitcast.388), calls=%async_computation.17 | async-start | bytes 8388608
  177.5 32.5 %copy-start.17 = (f32[512,1024]{1,0:T(8,128)}, f32[512,1024]{1,0:T(8,128)S(1)}, u32[]{:S(2)}) copy-start(f32[512,1024]{1,0:T(8,128)S(1)} %get-tuple-element.54) | copy-start | bytes 6291460
  177.9 10.8 %copy-start.25 = (bf16[1,512,1024]{2,1,0:T(8,128)(2,1)S(1)}, bf16[1,512,1024]{2,1,0:T(8,128)(2,1)}, u32[]{:S(2)}) copy-start(bf16[1,512,1024]{2,1,0:T(8,128)(2,1)} %param.23) | copy-start | bytes 3145732
  177.9 10.8 %slice-start.5 = ((s8[8388608]{0:T(1024)(128)(4,1)}), s8[4194304]{0:T(1024)(128)(4,1)S(1)}, s32[]{:S(2)}) async-start(s8[8388608]{0:T(1024)(128)(4,1)} %bitcast.388), calls=%async_computation.18 | async-start | bytes 8388608
  200.6 9.5 %copy-start.56 = (bf16[512,4096]{1,0:T(8,128)(2,1)}, bf16[512,4096]{1,0:T(8,128)(2,1)S(1)}, u32[]{:S(2)}) copy-start(bf16[512,4096]{1,0:T(8,128)(2,1)S(1)} %fusion.11) | copy-start | bytes 12582916
  210.8 5.9 copy-start.47
  216.7 238.5 %reduce-scatter.5.cloned.1.call-start = ((), (), s32[]{:S(2)}) async-start(), calls=%async_computation.8 | async-start | bytes 13369344 | tf_op jit(solution)/shard_map/reduce_scatter | solution.py:326
  222.1 7.2 slice-start
  222.2 7.8 slice-start.1
  222.2 8.5 slice-start.2
  234.2 6.9 copy-start.31
  252.0 368.9 %reduce-scatter.9.cloned.1.call-start = ((), (), s32[]{:S(2)}) async-start(), calls=%async_computation.10 | async-start | bytes 17825792 | tf_op jit(solution)/shard_map/reduce_scatter | solution.py:329
  264.4 538.6 %reduce-scatter.11.cloned.1.call-start = ((), (), s32[]{:S(2)}) async-start(), calls=%async_computation.11 | async-start | bytes 17825792 | tf_op jit(solution)/shard_map/reduce_scatter | solution.py:330
  284.3 3.6 collective-permute-start.1
  288.7 23.7 %all-to-all-start.2 = ((bf16[16,64,128]{2,1,0:T(8,128)(2,1)}), bf16[16,64,128]{2,1,0:T(8,128)(2,1)S(1)}, u32[]{:S(2)}, u32[]{:S(2)}) async-start(bf16[16,64,128]{2,1,0:T(8,128)(2,1)} %bitcast.379), calls=%async_computation.2 | async-start | bytes 524288 | tf_op jit(solution)/shard_map/all_to_all | solution.py:296
  298.5 14.9 %copy-start.27 = (f32[128,128]{0,1:T(8,128)S(1)}, f32[128,128]{0,1:T(8,128)}, u32[]{:S(2)}) copy-start(f32[128,128]{0,1:T(8,128)} %copy-done.26) | copy-start | bytes 196612
  315.8 10.9 %copy-start.3 = (f32[64,128,128]{2,1,0:T(8,128)}, f32[64,128,128]{2,1,0:T(8,128)S(1)}, u32[]{:S(2)}) copy-start(f32[64,128,128]{2,1,0:T(8,128)S(1)} %convolution_add_fusion.6) | copy-start | bytes 12582916
  316.8 9.9 %copy-start.4 = (f32[64,128,128]{2,1,0:T(8,128)}, f32[64,128,128]{2,1,0:T(8,128)S(1)}, u32[]{:S(2)}) copy-start(f32[64,128,128]{2,1,0:T(8,128)S(1)} %add_negate_fusion) | copy-start | bytes 12582916
  372.5 77.5 %all-to-all-start.3 = ((bf16[64,16,512]{2,0,1:T(8,128)(2,1)}), bf16[64,16,512]{2,0,1:T(8,128)(2,1)}, u32[]{:S(2)}, u32[]{:S(2)}) async-start(bf16[64,16,512]{2,0,1:T(8,128)(2,1)} %copy.312), calls=%async_computation.3 | async-start | bytes 2097152 | tf_op jit(solution)/shard_map/all_to_all | solution.py:318
  378.6 485.7 %all-reduce.9.cloned.1.call-start = ((), (), s32[]{:S(2)}) async-start(), calls=%async_computation.12 | async-start | bytes 3145728 | tf_op jit(solution)/shard_map/psum | solution.py:334
  397.3 43.3 %copy-start.44 = (f32[64,16]{1,0:T(8,128)S(1)}, f32[64,16]{1,0:T(8,128)}, u32[]{:S(2)}) copy-start(f32[64,16]{1,0:T(8,128)} %copy-done.43) | copy-start | bytes 12292
  440.7 9.2 %copy-start.36 = (f32[64,16]{1,0:T(8,128)S(1)}, f32[64,16]{1,0:T(8,128)}, u32[]{:S(2)}) copy-start(f32[64,16]{1,0:T(8,128)} %copy-done.35) | copy-start | bytes 12292
  440.7 9.2 %copy-start.38 = (f32[64,16]{1,0:T(8,128)S(1)}, f32[64,16]{1,0:T(8,128)}, u32[]{:S(2)}) copy-start(f32[64,16]{1,0:T(8,128)} %copy-done.37) | copy-start | bytes 12292
  805.1 8.2 copy-start.50
  805.1 9.5 %copy-start.46 = (f32[512]{0:T(512)S(1)}, f32[512]{0:T(512)}, u32[]{:S(2)}) copy-start(f32[512]{0:T(512)} %copy-done.45) | copy-start | bytes 6148
  805.1 10.4 %copy-start.52 = (f32[1024]{0:T(1024)S(1)}, f32[1024]{0:T(1024)}, u32[]{:S(2)}) copy-start(f32[1024]{0:T(1024)} %get-tuple-element.20) | copy-start | bytes 12292
  805.1 54.2 %copy-start.48 = (f32[512]{0:T(512)S(1)}, f32[512]{0:T(512)}, u32[]{:S(2)}) copy-start(f32[512]{0:T(512)} %copy-done.47) | copy-start | bytes 6148
  859.4 11.8 %copy-start.1 = (bf16[1024,1024]{1,0:T(8,128)(2,1)S(1)}, bf16[1024,1024]{1,0:T(8,128)(2,1)}, u32[]{:S(2)}) copy-start(bf16[1024,1024]{1,0:T(8,128)(2,1)} %param.19) | copy-start | bytes 6291460
  864.3 6.2 copy-start.39
  (26 other events, 68.5 us)
Sparse Core Ops, SparseCore 0:
  216.8 73.2 reduce-scatter.6
  294.7 143.6 reduce-scatter.4
  443.1 177.7 reduce-scatter.8
  625.4 177.5 reduce-scatter.10
  806.6 51.8 all-reduce.8
where the time goes:
time: 886 us; the launch traced here: 878 us
  matrix products  351 us (40%)
  waiting for transfers between devices  346 us (39%)
  other arithmetic  48.5 us (5%)
  local copies, waits for them, and re-layouts  41.8 us (5%)
  blocking collectives  41.3 us (5%)
  starting transfers between devices  33.6 us (4%)
  between operations  16 us (2%)
    reduce_scatter x1, waiting for transfers between devices, local(): lax.psum_scatter(reduce_grad, 'seq', scatter_dimension=0, tiled=True)  180 us
    reduce_scatter x1, waiting for transfers between devices, local(): lax.psum_scatter(expand_grad, 'seq', scatter_dimension=0, tiled=True)  164 us
    dot_general x24, matrix products, close_right(): jnp.einsum('ckn,nm->ckm', stacked, table, precision=triple, preferred_ele...  113 us
    dot_general x2, matrix products, lag_kernel(): jnp.einsum('cn,cnl->cl', weights * jnp.sqrt(decay_rates), jnp.exp(-decay_...  65 us
    dot_general x5, matrix products, inner_rows(): lax.dot_general(operand, partner, (((0,), (0,)), ((), ())), preferred_ele...  41.7 us
    dot_general x5, matrix products, against_rows(): lax.dot_general(operand, partner, (((1,), (1,)), ((), ())), preferred_ele...  37.4 us
    dot_general x5, matrix products, low_product(): return jnp.dot(operand, partner, preferred_element_type=jnp.float32)  36.8 us
    unnamed x1, blocking collectives  32 us
  transfers between devices with their start and end apart: 11, of which 4 were waited for; matrix products, arithmetic and copies ran while one was open for 35% of the time, Pallas kernels for 0%

commit v1 on v0

v1 whole, which is shorter than its diff:
```python
import functools
import heapq
import itertools
import math

import jax
import jax.numpy as jnp
from jax import lax
from jax.experimental import pallas as pl
from jax.experimental.pallas import tpu as pltpu
from jax.sharding import PartitionSpec as P


MESH=pl.DeviceIdType.MESH
BF=jnp.bfloat16

def sizes(nx, ns):
    ny = nx if ns % (2*nx)==0 else 1
    return {"x":nx,"y":ny,"z":ns//(2*ny)}

class Place:
    def __init__(s, n):
        s.n=n; q=lax.axis_index("seq")
        s.i=dict(x=lax.axis_index("grp"), y=lax.rem(lax.div(q,2),n["y"]), z=lax.div(q,2*n["y"])); s.c=lax.rem(q,2)
    def at(s, ax, k):
        return lax.rem(s.i[ax]+k, s.n[ax])
    def device(s, ax, k):
        j=dict(s.i); j[ax]=s.at(ax,k)
        return {"grp":j["x"],"seq":(j["z"]*s.n["y"]+j["y"])*2+s.c}
    def sibling(s):
        return {"seq":(s.i["z"]*s.n["y"]+s.i["y"])*2+1-s.c}
    def partners(s):
        return [s.device(ax,k) for ax in "xyz" for k in range(1,s.n[ax])]

def stage_shapes(n, order, rows, cw):
    left=dict(n); out=[]
    for ax in order:
        del left[ax]
        out.append(tuple(left[a] for a in "zy" if a in left)+(rows, cw*(left["x"] if "x" in left else 1)))
    return out

def piece_scratch(n, order, rows, cw):
    sh=stage_shapes(n,order,rows,cw)
    res=[]
    for ax,s in zip(order,sh):
        res.append(pltpu.VMEM((n[ax]-1,)+s,BF)); res.append(pltpu.VMEM(s,BF))
    most=max(n.values())-1
    res+= [pltpu.SemaphoreType.DMA((4,most)),pltpu.SemaphoreType.DMA((4,most))]
    return res

class Piece:
    def __init__(s, place, order, rows, cw, src, out, scratch):
        s.p,s.order,s.rows,s.cw,s.src,s.out=place,order,rows,cw,src,out
        s.recv=[scratch[0],scratch[2],scratch[4]]; s.sum=[scratch[1],scratch[3],scratch[5]]
        s.ss,s.rs=scratch[6],scratch[7]
        s.copies={}
    def view(s, stage, fixed):
        if stage==0:
            ref=s.src; lead=[fixed.get(a,slice(None)) for a in "zy"]; left=["z","y","x"]
        else:
            ref=s.sum[stage-1]; left=[a for a in "zyx" if a not in s.order[:stage]]
            lead=[fixed.get(a,slice(None)) for a in "zy" if a in left]
        cols=slice(None)
        if "x" in fixed and "x" in left: cols=pl.ds(pl.multiple_of(fixed["x"]*s.cw,128),s.cw)
        return ref, tuple(lead)+(slice(None),cols)
    def start(s, stage):
        if stage<3:
            ax=s.order[stage]
            for k in range(1,s.p.n[ax]):
                if stage==0: src=s.src(ax,s.p.at(ax,k))
                else:
                    ref,ix=s.view(stage,{ax:s.p.at(ax,k)}); src=ref.at[ix]
                cp=pltpu.make_async_remote_copy(src_ref=src,dst_ref=s.recv[stage].at[k-1],send_sem=s.ss.at[stage,k-1],recv_sem=s.rs.at[stage,k-1],device_id=s.p.device(ax,k),device_id_type=MESH)
                cp.start(); s.copies[stage,k]=cp
        else:
            for k in range(1,s.p.n["x"]):
                cp=pltpu.make_async_remote_copy(src_ref=s.sum[2],dst_ref=s.out.at[:,pl.ds(pl.multiple_of(s.p.i["x"]*s.cw,128),s.cw)],send_sem=s.ss.at[3,k-1],recv_sem=s.rs.at[3,k-1],device_id=s.p.device("x",k),device_id_type=MESH)
                cp.start(); s.copies[3,k]=cp
    def wait_send(s, stage):
        for (st,k),cp in s.copies.items():
            if st==stage: cp.wait_send()
    def finish(s, stage):
        for (st,k),cp in s.copies.items():
            if st==stage: cp.wait_recv()
        if stage==3: return
        ax=s.order[stage]; n=s.p.n
        left=[a for a in "zy" if a not in s.order[:stage+1]]
        R=s.recv[stage]; T=s.sum[stage]
        step=min(s.rows,32)
        for lead in itertools.product(*[range(n[a]) for a in left]):
            fixed=dict(zip(left,lead)); fixed[ax]=s.p.i[ax]
            if stage==0: own=s.src(None,None,fixed)
            else:
                ref,ix=s.view(stage,fixed); own=ref.at[ix]
            def body(r,_):
                rr=pl.ds(pl.multiple_of(r*step,16),step)
                v=own[rr,:].astype(jnp.float32)
                for k in range(n[ax]-1):
                    v=v+R[(k,)+lead+(rr,slice(None))].astype(jnp.float32)
                T[lead+(rr,slice(None))]=v.astype(BF)
                if stage==2:
                    s.out[rr,pl.ds(pl.multiple_of(s.p.i["x"]*s.cw,128),s.cw)]=v.astype(BF)
                return 0
            if s.rows==step: body(0,0)
            else: lax.fori_loop(0,s.rows//step,body,0)

def source(ref, place, rows0, rows, col0, cw):
    n=place.n
    def src(ax,j,fixed=None):
        fixed=dict(fixed or {})
        if ax: fixed[ax]=j
        lead=[fixed.get(a,slice(None)) for a in "zy"]
        if "x" in fixed: cols=pl.ds(pl.multiple_of(col0+fixed["x"]*cw,128),cw)
        else: cols=pl.ds(col0,cw*n["x"])
        return ref.at[tuple(lead)+(pl.ds(rows0,rows),cols)]
    return src

def barrier(place, extra=()):
    sem=pltpu.get_barrier_semaphore()
    ps=place.partners()+list(extra)
    for d in ps: pl.semaphore_signal(sem,inc=1,device_id=d,device_id_type=MESH)
    pl.semaphore_wait(sem,len(ps))

EPS=1e-5
BLK=512; CTX=128; HEADS=8; HD=128
F32=jnp.float32

def norm_rows(src, gain, dst, rows, step=64):
    def body(i,_):
        rr=pl.ds(pl.multiple_of(i*step,16),step)
        x=src[rr,:].astype(F32)
        x=x-jnp.mean(x,axis=-1,keepdims=True)
        v=jnp.mean(x*x,axis=-1,keepdims=True)
        dst[rr,:]=(x*lax.rsqrt(v+EPS)*gain).astype(BF)
        return 0
    lax.fori_loop(0,rows//step,body,0)

def rates(decay, length):
    return jnp.exp(decay)*(1.0/length)

def block_state(low, rate3, row0, rows, put):
    nst=rate3.shape[0]
    back=7.0-lax.broadcasted_iota(jnp.int32,(8,128),0).astype(F32)
    for lt in range(low.shape[1]//128):
        lanes=pl.ds(lt*128,128)
        r=[jnp.broadcast_to(rate3[n,lt:lt+1,:],(8,128)) for n in range(nst)]
        a8=[jnp.exp(-8.0*v) for v in r]
        def body(g,acc):
            u=low[pl.ds(pl.multiple_of(row0+g*16,16),16),lanes].astype(F32)
            lo,hi=u[:8],u[8:]
            acc=tuple(a*c+lo for a,c in zip(a8,acc))
            return tuple(a*c+hi for a,c in zip(a8,acc))
        acc=lax.fori_loop(0,rows//16,body,tuple(jnp.zeros((8,128),F32) for _ in range(nst)),unroll=2)
        for n in range(nst):
            put(n,lt,jnp.sum(acc[n]*jnp.exp(-back*r[n]),axis=0,keepdims=True))

def split_lanes(src, dst, rows):
    def body(g,_):
        for lt in range(src.shape[1]//128):
            v=src[pl.ds(pl.multiple_of(g*16,16),16),lt*128:(lt+1)*128].astype(F32)
            dst[pl.ds(g*16,16),lt,:]=v
        return 0
    lax.fori_loop(0,rows//16,body,0)

def join_lanes(src, dst, rows):
    def body(g,_):
        for lt in range(dst.shape[1]//128):
            dst[pl.ds(pl.multiple_of(g*16,16),16),lt*128:(lt+1)*128]=src[pl.ds(g*16,16),lt,:].astype(dst.dtype)
        return 0
    lax.fori_loop(0,rows//16,body,0)

class Scan:
    def __init__(s, ns, nst, s3, gather, spread, h3, sem, forward):
        s.ns,s.nst,s.s3,s.gather,s.spread,s.h3=ns,nst,s3,gather,spread,h3
        s.sem=sem; s.forward=forward; s.q=lax.axis_index("seq"); s.stride=ns//nst
        s.n=lax.div(s.q,s.stride); s.scans=lax.rem(s.q,s.stride)==0
    def to_scanner(s, n):
        return pltpu.make_async_remote_copy(src_ref=s.s3.at[n],dst_ref=s.gather.at[s.q],send_sem=s.sem[0].at[n],recv_sem=s.sem[1].at[s.q],device_id={"seq":n*s.stride},device_id_type=MESH)
    def from_block(s, b):
        return pltpu.make_async_remote_copy(src_ref=s.s3.at[0],dst_ref=s.gather.at[b],send_sem=s.sem[0].at[0],recv_sem=s.sem[1].at[b],device_id={"seq":b},device_id_type=MESH)
    def to_block(s, b):
        return pltpu.make_async_remote_copy(src_ref=s.spread.at[b],dst_ref=s.h3.at[s.n],send_sem=s.sem[2].at[b],recv_sem=s.sem[3].at[s.n],device_id={"seq":b},device_id_type=MESH)
    def from_scanner(s, n):
        return pltpu.make_async_remote_copy(src_ref=s.spread.at[0],dst_ref=s.h3.at[n],send_sem=s.sem[2].at[0],recv_sem=s.sem[3].at[n],device_id={"seq":n*s.stride},device_id_type=MESH)
    def each(s, count, fn, skip):
        def body(i,_):
            @pl.when(i!=skip)
            def _(): fn(i)
            return 0
        lax.fori_loop(0,count,body,0)
    def collect(s):
        mine=jnp.where(s.scans,s.n,s.nst)
        s.each(s.nst,lambda n:s.to_scanner(n).start(),mine)
    def scan(s, decay_block):
        mine=jnp.where(s.scans,s.n,s.nst)
        @pl.when(s.scans)
        def _():
            s.gather[s.q]=s.s3[s.n]
            s.each(s.ns,lambda b:s.from_block(b).wait_recv(),s.q)
            a=decay_block[s.n]
            def body(i,h):
                b=i if s.forward else s.ns-1-i
                s.spread[b]=h
                return a*h+s.gather[b]
            lax.fori_loop(0,s.ns,body,jnp.zeros((8,128),F32))
            s.each(s.ns,lambda b:s.to_block(b).start(),s.q)
            s.h3[s.n]=s.spread[s.q]
    def receive(s):
        mine=jnp.where(s.scans,s.n,s.nst)
        s.each(s.nst,lambda n:s.from_scanner(n).wait_recv(),mine)
    def drain(s):
        mine=jnp.where(s.scans,s.n,s.nst)
        s.each(s.nst,lambda n:s.to_scanner(n).wait_send(),mine)
        @pl.when(s.scans)
        def _(): s.each(s.ns,lambda b:s.to_block(b).wait_send(),s.q)

def scan_scratch(ns,nst):
    return [pltpu.VMEM((nst,8,128),F32),pltpu.VMEM((ns,8,128),F32),pltpu.VMEM((ns,8,128),F32),
      pltpu.SemaphoreType.DMA((nst,)),pltpu.SemaphoreType.DMA((ns,)),pltpu.SemaphoreType.DMA((ns,)),pltpu.SemaphoreType.DMA((nst,))]

def front_kernel(ns, length, x, cot, gain, decay3, weight3, w_hbm, low, tail_low, packed, ctx, pairs, h3, own3, cot_sib,
                 w, tail_x, rate3, dec3, u3, y3, s3, gather, spread, e0, e1, e2, e3, wsem, tsem, csem):
    q=lax.axis_index("seq"); c=lax.rem(q,2); g=lax.axis_index("grp")
    nst=decay3.shape[0]
    sem=pltpu.get_barrier_semaphore()
    def sig(i,_):
        @pl.when(i!=q)
        def _(): pl.semaphore_signal(sem,inc=1,device_id={"seq":i},device_id_type=MESH)
        return 0
    lax.fori_loop(0,ns,sig,0)
    wcp=pltpu.make_async_copy(w_hbm,w,wsem); wcp.start()
    pl.semaphore_wait(sem,ns-1)
    tail=pltpu.make_async_remote_copy(src_ref=x.at[pl.ds(BLK-CTX,CTX),:],dst_ref=tail_x,send_sem=tsem.at[0],recv_sem=tsem.at[1],device_id={"seq":jnp.minimum(q+1,ns-1)},device_id_type=MESH)
    @pl.when(q<ns-1)
    def _(): tail.start()
    cc=pltpu.make_async_remote_copy(src_ref=cot,dst_ref=cot_sib,send_sem=csem.at[0],recv_sem=csem.at[1],device_id={"seq":q+1-2*c},device_id_type=MESH)
    cc.start()
    rate3[...]=rates(decay3[...],length)
    dec3[...]=jnp.exp(-float(BLK)*rate3[...])
    norm_rows(x,gain[...],low,BLK)
    def put_own(n,lt,v): own3[n,lt:lt+1,:]=v
    block_state(low,rate3,0,BLK-CTX,put_own)
    @pl.when(q>0)
    def _(): tail.wait_recv()
    @pl.when(q==0)
    def _(): tail_x[...]=jnp.zeros_like(tail_x)
    norm_rows(tail_x,gain[...],tail_low,CTX)
    def put_tail(n,lt,v): s3[n,lt:lt+1,:]=v
    block_state(tail_low,rate3,0,CTX,put_tail)
    for n in range(nst):
        s3[n]=jnp.exp(-float(BLK-CTX)*rate3[n])*s3[n]+own3[n]
    ex=Scan(ns,nst,s3,gather,spread,h3,[e0,e1,e2,e3],True)
    ex.collect()
    wcp.wait()
    def mm(i,_):
        cols=pl.ds(pl.multiple_of(i*256,128),256)
        packed[:,cols]=jnp.dot(low[...],w[:,cols],preferred_element_type=F32).astype(BF)
        return 0
    tiles=packed.shape[1]//256
    lax.fori_loop(0,tiles//2,mm,0)
    ex.scan(dec3)
    split_lanes(tail_low,u3,CTX)
    lax.fori_loop(tiles//2,tiles,mm,0)
    ex.receive()
    a=[jnp.exp(-rate3[n]) for n in range(nst)]
    k=[weight3[n]*jnp.sqrt(rate3[n]) for n in range(nst)]
    def step(t,h):
        u=u3[t]
        h=tuple(p*v+u for p,v in zip(a,h))
        ys=[p*v for p,v in zip(k,h)]
        while len(ys)>1: ys=[ys[i]+ys[i+1] if i+1<len(ys) else ys[i] for i in range(0,len(ys),2)]
        y3[t]=ys[0]
        return h
    lax.fori_loop(0,CTX,step,tuple(h3[n] for n in range(nst)),unroll=2)
    join_lanes(y3,ctx,CTX)
    d=low.shape[1]
    def pm(i,_):
        cols=pl.ds(pl.multiple_of(i*256,128),256)
        pairs[:,cols]=jnp.dot(ctx[...],w[:,pl.ds(pl.multiple_of(d+i*256,128),256)],preferred_element_type=F32).astype(BF)
        return 0
    lax.fori_loop(0,pairs.shape[1]//256,pm,0)
    ex.drain()
    @pl.when(q<ns-1)
    def _(): tail.wait_send()
    cc.wait()

def front(ns, x, cot, gain, decay3, weight3, w):
    nst=decay3.shape[0]; d=x.shape[1]
    V=pl.BlockSpec(memory_space=pltpu.VMEM); A=pl.BlockSpec(memory_space=pl.ANY)
    S=lambda *s,t=BF: jax.ShapeDtypeStruct(s,t)
    return pl.pallas_call(functools.partial(front_kernel,ns,x.shape[0]*ns),
        out_shape=[S(BLK,d),S(CTX,d),S(BLK,3*d),S(CTX,d),S(CTX,2*d),S(nst,8,128,t=F32),S(nst,8,128,t=F32),S(BLK,d)],
        in_specs=[V,A,V,V,V,A],out_specs=[V]*7+[A],
        scratch_shapes=[pltpu.VMEM((d,3*d),BF),pltpu.VMEM((CTX,d),BF),pltpu.VMEM((nst,8,128),F32),pltpu.VMEM((nst,8,128),F32),
          pltpu.VMEM((CTX,8,128),F32),pltpu.VMEM((CTX,8,128),F32)]+scan_scratch(ns,nst)+[pltpu.SemaphoreType.DMA,pltpu.SemaphoreType.DMA((2,)),pltpu.SemaphoreType.DMA((2,))],
        compiler_params=pltpu.CompilerParams(collective_id=0,has_side_effects=True,vmem_limit_bytes=60*2**20),
        name="front")(x,cot,gain,decay3,weight3,w)

NEG=-1e30
NT=(((1,),(1,)),((),()))
TN=(((0,),(0,)),((),()))
NN=(((1,),(0,)),((),()))
def mm(a,b,dims=NN): return lax.dot_general(a,b,dims,preferred_element_type=F32)

def attention_kernel(q,k,v,ck,cv,seg,vis,x,wo,gain,probs,attended,residual,low2,bias):
    h=pl.program_id(0)
    @pl.when(h==0)
    def _():
        row=jnp.broadcast_to(seg[...].astype(F32),(128,BLK))
        col=jnp.transpose(row)
        def body(i,_):
            rr=pl.ds(pl.multiple_of(i*128,128),128)
            qi=i*128+lax.broadcasted_iota(jnp.int32,(128,BLK),0)
            kj=lax.broadcasted_iota(jnp.int32,(128,BLK),1)
            return 0
        for i in range(BLK//128):
            ci=col[i*128:(i+1)*128]
            for j in range(BLK//128):
                if j>i:
                    bias[i*128:(i+1)*128,j*128:(j+1)*128]=jnp.full((128,128),NEG,F32); continue
                ok=ci==row[:,j*128:(j+1)*128]
                if i==j: ok=ok&(lax.broadcasted_iota(jnp.int32,(128,128),0)>=lax.broadcasted_iota(jnp.int32,(128,128),1))
                bias[i*128:(i+1)*128,j*128:(j+1)*128]=jnp.where(ok,0.0,NEG)
        bias[:,BLK:]=jnp.broadcast_to(vis[...],(BLK,CTX))
    scale=1.0/math.sqrt(HD)
    half=BLK//2
    for r in range(2):
        rows=slice(r*half,(r+1)*half); n=(r+1)*half
        s1=mm(q[rows,:],k[:n,:],NT)*scale+bias[rows,:n]
        s2=mm(q[rows,:],ck[...],NT)*scale+bias[rows,BLK:]
        top=jnp.maximum(jnp.max(s1,axis=-1,keepdims=True),jnp.max(s2,axis=-1,keepdims=True))
        e1=jnp.exp(s1-top); e2=jnp.exp(s2-top)
        inv=1.0/(jnp.sum(e1,axis=-1,keepdims=True)+jnp.sum(e2,axis=-1,keepdims=True))
        p1=(e1*inv).astype(BF); p2=(e2*inv).astype(BF)
        probs[0,rows,:n]=p1; probs[0,rows,BLK:]=p2
        if n<BLK: probs[0,rows,n:BLK]=jnp.zeros((half,BLK-n),BF)
        o=mm(p1,v[:n,:])+mm(p2,cv[...])
        attended[rows,pl.ds(pl.multiple_of(h*HD,HD),HD)]=o.astype(BF)
    @pl.when(h==HEADS-1)
    def _():
        def body(i,_):
            rr=pl.ds(pl.multiple_of(i*128,128),128)
            res=x[rr,:].astype(F32)+mm(attended[rr,:],wo[...])
            residual[rr,:]=res
            m=res-jnp.mean(res,axis=-1,keepdims=True)
            var=jnp.mean(m*m,axis=-1,keepdims=True)
            low2[rr,:]=(m*lax.rsqrt(var+EPS)*gain[...]).astype(BF)
            return 0
        lax.fori_loop(0,BLK//128,body,0)

def attention(packed,pairs,seg,vis,x,wo,gain):
    d=x.shape[1]
    S=lambda *s,t=BF: jax.ShapeDtypeStruct(s,t)
    full=lambda a: pl.BlockSpec(a.shape,lambda h:(0,)*a.ndim)
    return pl.pallas_call(attention_kernel,grid=(HEADS,),
      in_specs=[pl.BlockSpec((BLK,HD),lambda h:(0,h)),pl.BlockSpec((BLK,HD),lambda h:(0,HEADS+h)),pl.BlockSpec((BLK,HD),lambda h:(0,2*HEADS+h)),
        pl.BlockSpec((CTX,HD),lambda h:(0,h)),pl.BlockSpec((CTX,HD),lambda h:(0,HEADS+h)),full(seg),full(vis),full(x),full(wo),full(gain)],
      out_specs=[pl.BlockSpec((1,BLK,BLK+CTX),lambda h:(h,0,0)),pl.BlockSpec((BLK,d),lambda h:(0,0)),pl.BlockSpec((BLK,d),lambda h:(0,0)),pl.BlockSpec((BLK,d),lambda h:(0,0))],
      out_shape=[S(HEADS,BLK,BLK+CTX),S(BLK,d),S(BLK,d,t=F32),S(BLK,d)],
      scratch_shapes=[pltpu.VMEM((BLK,BLK+CTX),F32)],
      compiler_params=pltpu.CompilerParams(vmem_limit_bytes=48*2**20),
      cost_estimate=pl.CostEstimate(flops=4*10**9,bytes_accessed=2*10**7,transcendentals=3*10**6),
      name="attention")(packed,packed,packed,pairs,pairs,seg,vis,x,wo,gain)

G0=math.sqrt(2/math.pi); G1=0.044715
def gelu_pair(h):
    h2=h*h
    th=jnp.tanh(h*(G0+G0*G1*h2))
    p=0.5*(1.0+th)
    return h*p, p+h*(0.5*(1.0-th*th))*(G0+3*G0*G1*h2)

def ffn_kernel(n, nff, xo, coto, cots, w1, w2, A, B, out_own, out_rec, dx_own, dx_rec,
               x2, x2t, cot2, w1s, w2s, act, dexp, sbuf, wsem1, wsem2, xsem, osem, dsem):
    place=Place(n); c=place.c; sib=place.sibling()
    tiles=w1s.shape[1]//256; d=xo.shape[1]; rf=A.shape[2]
    sem=pltpu.get_barrier_semaphore()
    pl.semaphore_signal(sem,inc=1,device_id=sib,device_id_type=MESH)
    if rf%128==0:
        per=256//rf if rf<256 else 1; wd=min(rf,256)
        def cp(i):
            j=i*wd
            src=lax.div(j,rf)*(2*rf)+c*rf+lax.rem(j,rf)
            return (pltpu.make_async_copy(w1.at[:,pl.ds(pl.multiple_of(src,128),wd)],w1s.at[:,pl.ds(pl.multiple_of(j,128),wd)],wsem1.at[i]),
                    pltpu.make_async_copy(w2.at[pl.ds(pl.multiple_of(src,16),wd),:],w2s.at[pl.ds(pl.multiple_of(j,16),wd),:],wsem2.at[i]))
    else:
        per=1; wd=256
        def cp(i):
            j=i*wd
            return (pltpu.make_async_copy(w1.at[:,pl.ds(pl.multiple_of(j,128),wd)],w1s.at[:,pl.ds(pl.multiple_of(j,128),wd)],wsem1.at[i]),
                    pltpu.make_async_copy(w2.at[pl.ds(pl.multiple_of(j,16),wd),:],w2s.at[pl.ds(pl.multiple_of(j,16),wd),:],wsem2.at[i]))
    count=tiles*256//wd
    def go(i,_):
        a,b=cp(i); a.start(); b.start(); return 0
    lax.fori_loop(0,count,go,0)
    pl.semaphore_wait(sem,1)
    xs=pltpu.make_async_remote_copy(src_ref=xo,dst_ref=x2.at[pl.ds(BLK,BLK),:],send_sem=xsem.at[0],recv_sem=xsem.at[1],device_id=sib,device_id_type=MESH)
    xs.start()
    x2[0:BLK,:]=xo[...]
    cot2[0:BLK,:]=coto[...]; cot2[BLK:,:]=cots[...]
    for i in range(d//256): x2t[i*256:(i+1)*256,0:BLK]=jnp.transpose(xo[:,i*256:(i+1)*256])
    xs.wait()
    for i in range(d//256): x2t[i*256:(i+1)*256,BLK:]=jnp.transpose(x2[BLK:,i*256:(i+1)*256])
    def tile(t,_):
        for j in range(per):
            a,b=cp(t*per+j); a.wait(); b.wait()
        cols=pl.ds(pl.multiple_of(t*256,256),256)
        def part(r,_):
            rr=pl.ds(pl.multiple_of(r*256,256),256)
            h=mm(x2[rr,:],w1s[:,cols]); u=mm(cot2[rr,:],w2s[cols,:],NT)
            a,g=gelu_pair(h)
            act[rr,cols]=a.astype(BF); dexp[rr,cols]=(u*g).astype(BF)
            return 0
        lax.fori_loop(0,2*BLK//256,part,0)
        def ga(k,_):
            kc=pl.ds(pl.multiple_of(k*256,256),256)
            v=mm(act[:,cols],cot2[:,kc],TN).astype(BF)
            for j in range(max(1,256//rf)):
                zy=lax.div(t*256,rf)+j; w=min(rf,256)
                A[lax.div(zy,n["y"]),lax.rem(zy,n["y"]),pl.ds(pl.multiple_of(lax.rem(t*256,rf),16),w) if rf>256 else slice(None),kc]=v[j*w:(j+1)*w]
            return 0
        lax.fori_loop(0,d//256,ga,0)
        rb=B.shape[2]; nzy=n["z"]*n["y"]; group=max(1,256//rb)
        def gb(k,_):
            rr=pl.ds(pl.multiple_of(k*group*rb,16),group*rb)
            v=mm(x2t[rr,:],dexp[:,cols]).astype(BF)
            for j in range(group):
                zy=k*group+j
                B[lax.div(zy,n["y"]),lax.rem(zy,n["y"]),:,cols]=v[j*rb:(j+1)*rb]
            return 0
        lax.fori_loop(0,nzy//group,gb,0)
        return 0
    lax.fori_loop(0,tiles,tile,0)
    def dx(r,dst):
        rr=pl.ds(pl.multiple_of(r*256,256),256)
        return mm(dexp[rr,:],w1s[...],NT)
    def ou(r):
        rr=pl.ds(pl.multiple_of(r*256,256),256)
        return mm(act[rr,:],w2s[...])
    for r in range(2):
        sbuf[0,r*256:(r+1)*256,:]=dx(2+r,None).astype(BF)
    dc=pltpu.make_async_remote_copy(src_ref=sbuf.at[0],dst_ref=dx_rec,send_sem=dsem.at[0],recv_sem=dsem.at[1],device_id=sib,device_id_type=MESH); dc.start()
    for r in range(2):
        sbuf[1,r*256:(r+1)*256,:]=ou(2+r).astype(BF)
    oc=pltpu.make_async_remote_copy(src_ref=sbuf.at[1],dst_ref=out_rec,send_sem=osem.at[0],recv_sem=osem.at[1],device_id=sib,device_id_type=MESH); oc.start()
    for r in range(2):
        dx_own[r*256:(r+1)*256,:]=dx(r,None)
        out_own[r*256:(r+1)*256,:]=ou(r)
    dc.wait(); oc.wait()

def ffn(n, xo, coto, cots, w1, w2):
    d=xo.shape[1]; ff=w1.shape[1]; zy=n["z"]*n["y"]; own=ff//2; rf=own//zy; rb=d//zy
    V=pl.BlockSpec(memory_space=pltpu.VMEM); Y=pl.BlockSpec(memory_space=pl.ANY)
    S=lambda *s,t=BF: jax.ShapeDtypeStruct(s,t)
    if rf%128:
        c=lax.rem(lax.axis_index("seq"),2)
        w1=lax.dynamic_index_in_dim(w1.reshape(d,zy,2,rf),c,2,keepdims=False).reshape(d,own)
        w2=lax.dynamic_index_in_dim(w2.reshape(zy,2,rf,d),c,1,keepdims=False).reshape(own,d)
    D=pltpu.SemaphoreType.DMA; nc=own//min(max(rf,128),256) if rf%128==0 else own//256
    return pl.pallas_call(functools.partial(ffn_kernel,n,ff),
      out_shape=[S(n["z"],n["y"],rf,d),S(n["z"],n["y"],rb,own),S(BLK,d,t=F32),S(BLK,d),S(BLK,d,t=F32),S(BLK,d)],
      in_specs=[V,V,V,Y,Y],out_specs=[V]*6,
      scratch_shapes=[pltpu.VMEM((2*BLK,d),BF),pltpu.VMEM((d,2*BLK),BF),pltpu.VMEM((2*BLK,d),BF),pltpu.VMEM((d,own),BF),pltpu.VMEM((own,d),BF),
        pltpu.VMEM((2*BLK,own),BF),pltpu.VMEM((2*BLK,own),BF),pltpu.VMEM((2,BLK,d),BF),D((nc,)),D((nc,)),D((2,)),D((2,)),D((2,))],
      compiler_params=pltpu.CompilerParams(collective_id=1,has_side_effects=True,vmem_limit_bytes=60*2**20),
      cost_estimate=pl.CostEstimate(flops=26*10**9,bytes_accessed=3*10**7,transcendentals=2*10**6),
      name="ffn")(xo,coto,cots,w1,w2)


def norm_back(v, gain, dy):
    x=v-jnp.mean(v,axis=-1,keepdims=True)
    s=lax.rsqrt(jnp.mean(x*x,axis=-1,keepdims=True)+EPS)
    nrm=x*s
    dn=dy*gain
    dv=(dn-jnp.mean(dn,axis=-1,keepdims=True)-nrm*jnp.mean(dn*nrm,axis=-1,keepdims=True))*s
    return dv, dy*nrm
def fold(v):
    return jnp.sum(v.reshape(v.shape[0]//8,8,v.shape[1]),axis=0)

def middle_kernel(dx_own,dx_rec,residual,gain,cot,attended,wo,out_own,out_rec, out,rgrad,branch,ggrad,agrad):
    ggrad[...]=jnp.zeros_like(ggrad)
    def body(i,_):
        rr=pl.ds(pl.multiple_of(i*64,64),64)
        dy=dx_own[rr,:]+dx_rec[rr,:].astype(F32)
        dv,g=norm_back(residual[rr,:],gain[...],dy)
        r=cot[rr,:].astype(F32)+dv
        rgrad[rr,:]=r; b=r.astype(BF); branch[rr,:]=b
        ggrad[...]+=fold(g)
        out[rr,:]=(residual[rr,:]+out_own[rr,:]+out_rec[rr,:].astype(F32)).astype(BF)
        return 0
    lax.fori_loop(0,BLK//64,body,0)
    def ag(i,_):
        rr=pl.ds(pl.multiple_of(i*256,256),256)
        agrad[rr,:]=mm(branch[rr,:],wo[...],NT).astype(BF)
        return 0
    lax.fori_loop(0,BLK//256,ag,0)

def call(kernel, ins, outs, scratch=(), name=None, flops=10**9, **kw):
    V=pl.BlockSpec(memory_space=pltpu.VMEM)
    return pl.pallas_call(kernel,out_shape=outs,in_specs=[V]*len(ins),out_specs=[V]*len(outs),scratch_shapes=list(scratch),
      compiler_params=pltpu.CompilerParams(vmem_limit_bytes=60*2**20,**kw),cost_estimate=pl.CostEstimate(flops=flops,bytes_accessed=2*10**7,transcendentals=0),name=name)(*ins)
def S(*s,t=BF): return jax.ShapeDtypeStruct(s,t)

def attention_back_kernel(q,k,v,ck,cv,p,o,do,dq,dk,dv,dck,dcv):
    scale=1.0/math.sqrt(HD)
    half=BLK//2
    for r in range(2):
        rows=slice(r*half,(r+1)*half); n=(r+1)*half
        g=do[rows,:]
        dot=jnp.sum(g.astype(F32)*o[rows,:].astype(F32),axis=-1,keepdims=True)
        p1=p[0,rows,:n]; p2=p[0,rows,BLK:]
        s1=(p1.astype(F32)*(mm(g,v[:n,:],NT)-dot)).astype(BF)
        s2=(p2.astype(F32)*(mm(g,cv[...],NT)-dot)).astype(BF)
        dq[rows,:]=((mm(s1,k[:n,:])+mm(s2,ck[...]))*scale).astype(BF)
        qr=q[rows,:]
        a1=mm(s1,qr,TN)*scale; a2=mm(s2,qr,TN)*scale; b1=mm(p1,g,TN); b2=mm(p2,g,TN)
        if r==0: first=(a1,a2,b1,b2)
    dk[0:half,:]=(first[0]+a1[:half]).astype(BF); dk[half:,:]=a1[half:].astype(BF)
    dv[0:half,:]=(first[2]+b1[:half]).astype(BF); dv[half:,:]=b1[half:].astype(BF)
    dck[...]=(first[1]+a2).astype(BF); dcv[...]=(first[3]+b2).astype(BF)

def attention_back(packed,pairs,probs,attended,agrad):
    d=attended.shape[1]
    col=lambda n,o: pl.BlockSpec((n,HD),lambda h,o=o:(0,o+h))
    return pl.pallas_call(attention_back_kernel,grid=(HEADS,),
      in_specs=[col(BLK,0),col(BLK,HEADS),col(BLK,2*HEADS),col(CTX,0),col(CTX,HEADS),pl.BlockSpec((1,BLK,BLK+CTX),lambda h:(h,0,0)),col(BLK,0),col(BLK,0)],
      out_specs=[col(BLK,0)]*3+[col(CTX,0)]*2,out_shape=[S(BLK,d)]*3+[S(CTX,d)]*2,
      compiler_params=pltpu.CompilerParams(vmem_limit_bytes=48*2**20),
      cost_estimate=pl.CostEstimate(flops=4*10**9,bytes_accessed=2*10**7,transcendentals=0),
      name="attention_back")(packed,packed,packed,pairs,pairs,probs,attended,agrad)

def grads_kernel(low,ctx,dq,dk,dv,dck,dcv,attended,branch,w, C,G,dn, lt,ct,at):
    d=low.shape[1]; nz,ny=C.shape[0],C.shape[1]; rb=C.shape[3]; per=256//rb
    def tr(i,_):
        cols=pl.ds(pl.multiple_of(i*256,256),256)
        lt[cols,:]=jnp.transpose(low[:,cols]); ct[cols,:]=jnp.transpose(ctx[:,cols]); at[cols,:]=jnp.transpose(attended[:,cols])
        return 0
    lax.fori_loop(0,d//256,tr,0)
    def put(i,v,col0):
        for j in range(per):
            b=i*per+j; zy=lax.div(b,2)
            C[lax.div(zy,ny),lax.rem(zy,ny),lax.rem(b,2),:,col0:col0+d]=v[j*rb:(j+1)*rb].astype(BF)
    def rows(i,_):
        rr=pl.ds(pl.multiple_of(i*256,256),256)
        put(i,mm(lt[rr,:],dq[...]),0)
        put(i,mm(lt[rr,:],dk[...])+mm(ct[rr,:],dck[...]),d)
        put(i,mm(lt[rr,:],dv[...])+mm(ct[rr,:],dcv[...]),2*d)
        put(i,mm(at[rr,:],branch[...]),3*d)
        return 0
    lax.fori_loop(0,d//256,rows,0)
    G[...]=(mm(dck[...],w[:,d:2*d],NT)+mm(dcv[...],w[:,2*d:],NT)).astype(BF)
    def back(i,_):
        rr=pl.ds(pl.multiple_of(i*256,256),256)
        dn[rr,:]=mm(dq[rr,:],w[:,:d],NT)+mm(dk[rr,:],w[:,d:2*d],NT)+mm(dv[rr,:],w[:,2*d:],NT)
        return 0
    lax.fori_loop(0,BLK//256,back,0)

def conv_back_kernel(ns,length,G,tail_low,low,decay3,weight3,h3, sig,kwg,kdg, rate3,dec3,u3,g3,y3,hb,sp3,d0,d1,tailb,tail_in,s3,gather,spread,e0,e1,e2,e3,tsem):
    q=lax.axis_index("seq"); nst=decay3.shape[0]
    sem=pltpu.get_barrier_semaphore()
    def sg(i,_):
        @pl.when(i!=q)
        def _(): pl.semaphore_signal(sem,inc=1,device_id={"seq":i},device_id_type=MESH)
        return 0
    lax.fori_loop(0,ns,sg,0)
    rate3[...]=rates(decay3[...],length)
    dec3[...]=jnp.exp(-float(BLK)*rate3[...])
    split_lanes(G,g3,CTX)
    a=[jnp.exp(-rate3[n]) for n in range(nst)]
    k=[weight3[n]*jnp.sqrt(rate3[n]) for n in range(nst)]
    def back(i,g):
        t=CTX-1-i
        v=g3[t]
        g=tuple(p*x+v for p,x in zip(a,g))
        ys=[p*x for p,x in zip(k,g)]
        while len(ys)>1: ys=[ys[i]+ys[i+1] for i in range(0,len(ys),2)]
        y3[t]=ys[0]
        return g
    g=lax.fori_loop(0,CTX,back,tuple(jnp.zeros((8,128),F32) for _ in range(nst)),unroll=2)
    for n in range(nst): s3[n]=g[n]
    pl.semaphore_wait(sem,ns-1)
    ex=Scan(ns,nst,s3,gather,spread,hb,[e0,e1,e2,e3],False)
    ex.collect()
    split_lanes(tail_low,u3,CTX)
    up=lax.broadcasted_iota(jnp.int32,(8,128),0).astype(F32)
    for lt in range(low.shape[1]//128):
        lanes=pl.ds(lt*128,128)
        for part in range(0,nst,8):
            r=[jnp.broadcast_to(rate3[n,lt:lt+1,:],(8,128)) for n in range(part,part+8)]
            a8=[jnp.exp(-8.0*v) for v in r]
            def body(i,cr):
                acc,der=cr
                u=low[pl.ds(pl.multiple_of(i*16,16),16),lanes].astype(F32)
                for w in (u[:8],u[8:]):
                    der=tuple(p*(x+y) for p,x,y in zip(a8,der,acc))
                    acc=tuple(p*y+w for p,y in zip(a8,acc))
                return acc,der
            z=tuple(jnp.zeros((8,128),F32) for _ in range(8))
            acc,der=lax.fori_loop(0,(BLK-CTX)//16,body,(z,z))
            for i,n in enumerate(range(part,part+8)):
                j=7.0-up
                sp3[n,lt:lt+1,:]=jnp.sum(jnp.exp(-j*r[i])*(8.0*der[i]+j*acc[i]),axis=0,keepdims=True)
    ex.scan(dec3)
    for part in range(0,nst,4):
        z=tuple(jnp.zeros((8,128),F32) for _ in range(4))
        def fwd(t,cr):
            h,hp,s0,s1=cr
            u=u3[t]; gg=g3[t]; aa=a[part:part+4]
            hp=tuple(p*(x+y) for p,x,y in zip(aa,hp,h))
            h=tuple(p*x+u for p,x in zip(aa,h))
            s0=tuple(x+gg*y for x,y in zip(s0,h)); s1=tuple(x+gg*y for x,y in zip(s1,hp))
            return h,hp,s0,s1
        h,hp,s0,s1=lax.fori_loop(0,CTX,fwd,(tuple(h3[n] for n in range(part,part+4)),z,z,z),unroll=2)
        for i,n in enumerate(range(part,part+4)):
            d0[n]=s0[i]; d1[n]=s1[i]
            m=float(BLK-CTX)
            am=jnp.exp(-m*rate3[n])
            sp3[n]=a[n]*(am*hp[i]+m*am*h[i]+sp3[n])
    ex.receive()
    for n in range(nst):
        r=rate3[n]; D1=d1[n]+hb[n]*sp3[n]; sq=jnp.sqrt(r)
        kwg[n]=sq*d0[n]
        kdg[n]=weight3[n]*sq*(0.5*d0[n]-r*D1)
    for lt in range(low.shape[1]//128):
        lanes=slice(lt*128,(lt+1)*128)
        r=[jnp.broadcast_to(rate3[n,lt:lt+1,:],(8,128)) for n in range(nst)]
        a8=[jnp.exp(-8.0*x) for x in r]
        v=tuple(jnp.broadcast_to((weight3[n,lt:lt+1,:]*jnp.sqrt(rate3[n,lt:lt+1,:]))*hb[n,lt:lt+1,:],(8,128))*jnp.exp(-(8.0-up)*r[n]) for n in range(nst))
        def total(v):
            ys=list(v)
            while len(ys)>1: ys=[ys[i]+ys[i+1] for i in range(0,len(ys),2)]
            return ys[0]
        def own(i,v):
            b=total(v); v=tuple(p*x for p,x in zip(a8,v))
            t=total(v); v=tuple(p*x for p,x in zip(a8,v))
            sig[pl.ds(pl.multiple_of(BLK-CTX-16-i*16,16),16),lanes]=jnp.concatenate([t,b],axis=0).astype(BF)
            return v
        v=lax.fori_loop(0,(BLK-CTX)//16,own,v)
        def tl(i,v):
            b=total(v); v=tuple(p*x for p,x in zip(a8,v))
            t=total(v); v=tuple(p*x for p,x in zip(a8,v))
            row=pl.multiple_of(CTX-16-i*16,16)
            tailb[pl.ds(row,16),lanes]=(jnp.concatenate([t,b],axis=0)+y3[pl.ds(row,16),lt,:]).astype(BF)
            return v
        lax.fori_loop(0,CTX//16,tl,v)
    back_copy=pltpu.make_async_remote_copy(src_ref=tailb,dst_ref=tail_in,send_sem=tsem.at[0],recv_sem=tsem.at[1],device_id={"seq":jnp.maximum(q-1,0)},device_id_type=MESH)
    @pl.when(q>0)
    def _(): back_copy.start()
    @pl.when(q==ns-1)
    def _(): tail_in[...]=jnp.zeros_like(tail_in)
    @pl.when(q<ns-1)
    def _(): back_copy.wait_recv()
    sig[BLK-CTX:,:]=tail_in[...]
    @pl.when(q>0)
    def _(): back_copy.wait_send()
    ex.drain()

def conv_back(ns,G,tail_low,low,decay3,weight3,h3):
    nst=decay3.shape[0]; d=low.shape[1]; M=pltpu.VMEM; st=(nst,8,128)
    return call(functools.partial(conv_back_kernel,ns,BLK*ns),[G,tail_low,low,decay3,weight3,h3],[S(BLK,d),S(*st,t=F32),S(*st,t=F32)],
      [M(st,F32),M(st,F32),M((CTX,8,128),F32),M((CTX,8,128),F32),M((CTX,8,128),F32),M(st,F32),M(st,F32),M(st,F32),M(st,F32),M((CTX,d),BF),M((CTX,d),BF)]+scan_scratch(ns,nst)+[pltpu.SemaphoreType.DMA((2,))],
      name="conv_back",collective_id=2,has_side_effects=True)

def last_kernel(x,gain,dn,sig,rgrad, igrad,ggrad):
    ggrad[...]=jnp.zeros_like(ggrad)
    def body(i,_):
        rr=pl.ds(pl.multiple_of(i*64,64),64)
        dv,g=norm_back(x[rr,:].astype(F32),gain[...],dn[rr,:]+sig[rr,:].astype(F32))
        igrad[rr,:]=rgrad[rr,:]+dv
        ggrad[...]+=fold(g)
        return 0
    lax.fori_loop(0,BLK//64,body,0)

def rs_kernel(n, plan, sched, A,B,Cf, OA,OB,OC, C,crec,csem,*scr):
    place=Place(n); c=place.c
    barrier(place,[place.sibling()])
    cps=[]
    nz,ny=n["z"],n["y"]
    for z in range(nz):
        cp=pltpu.make_async_remote_copy(src_ref=Cf.at[z,:,1-c],dst_ref=crec.at[z],send_sem=csem.at[0,z],recv_sem=csem.at[1,z],device_id=place.sibling(),device_id_type=MESH)
        cp.start(); cps.append(cp)
    T=[A,B,C]; O=[OA,OB,OC]
    pieces=[Piece(place,o,r,cw,source(T[t],place,r0,r,c0,cw),O[t].at[pl.ds(r0,r),pl.ds(c0,cw*n["x"])],scr[8*i:8*i+8]) for i,(t,r0,r,c0,cw,o) in enumerate(plan)]
    for i,p in enumerate(plan):
        if p[0]<2: pieces[i].start(0)
    rb=C.shape[2]
    for z in range(nz):
        cps[z].wait_recv()
        def add(y,_):
            for h in range(rb//16):
                rr=slice(h*16,h*16+16)
                C[z,y,rr,:]=(Cf[z,y,c,rr,:].astype(F32)+crec[z,y,rr,:].astype(F32)).astype(BF)
            return 0
        lax.fori_loop(0,ny,add,0)
    for i,p in enumerate(plan):
        if p[0]==2: pieces[i].start(0)
    for i,s in sched:
        pieces[i].finish(s)
        if s<3: pieces[i].start(s+1)
    for p in pieces:
        for s in range(4): p.wait_send(s)
    for cp in cps: cp.wait_send()

def simulate(n, plan, ready):
    free=dict(x=0.,y=0.,z=0.); res={}
    ev=[(ready[p[0]],i,0) for i,p in enumerate(plan)]; heapq.heapify(ev)
    while ev:
        t,i,s=heapq.heappop(ev)
        (_,r0,r,c0,cw,order)=plan[i]
        if s<3:
            ax=order[s]; shape=stage_shapes(n,order,r,cw)[s]; vol=math.prod(shape)*4*(n[ax]**2/4 if n[ax]>2 else 1)
        else: ax="x"; vol=r*cw*4
        st=max(t,free[ax]); en=st+vol/91e3; free[ax]=en
        res[i,s]=en+1.5
        if s<3: heapq.heappush(ev,(en+2.5,i,s+1))
    return sorted(res,key=lambda k:(res[k],k[1])), max(free.values())

def make_plan(n, ra, rb, rc, d, own, tot):
    nx=n["x"]; plan=[]
    def cut(t,rows,cols,orders):
        parts=len(orders)
        while rows//parts<16: parts//=2
        r=rows//parts
        for i in range(parts): plan.append((t,i*r,r,0,cols//nx,orders[i]))
    cut(0,ra,d,["xyz"]*4); cut(1,rb,own,["yxz"]*4); cut(2,rc,tot,["zxy","xyz","yxz","zxy"])
    return plan

def reduce_all(n, A,B,Cf):
    nz,ny=n["z"],n["y"]; ra,d=A.shape[2:]; rb,own=B.shape[2:]; rc,tot=Cf.shape[3:]
    plan=make_plan(n,ra,rb,rc,d,own,tot)
    sched,_=simulate(n,plan,[0.,0.,12.])
    scr=[pltpu.VMEM((nz,ny,rc,tot),BF),pltpu.VMEM((nz,ny,rc,tot),BF),pltpu.SemaphoreType.DMA((2,nz))]
    for (t,r0,r,c0,cw,o) in plan: scr+=piece_scratch(n,o,r,cw)
    return call(functools.partial(rs_kernel,n,plan,sched),[A,B,Cf],[S(ra,d),S(rb,own),S(rc,tot)],scr,name="reduce_all",collective_id=3,has_side_effects=True)

def local(layer_input,segment_ids,context_mask,first_gain,attention_in,kernel_weight,kernel_decay,attention_out,second_gain,expand_weight,reduce_weight,cotangent):
    ns=lax.axis_size("seq"); nx=lax.axis_size("grp"); nst=kernel_decay.shape[1]; n=sizes(nx,ns)
    q=lax.axis_index("seq"); c=lax.rem(q,2)
    x=layer_input[0]; cot=cotangent[0]; d=x.shape[1]; ff=expand_weight.shape[1]
    decay3=kernel_decay.T.reshape(nst,8,128); weight3=kernel_weight.T.reshape(nst,8,128)
    low,tail_low,packed,ctx,pairs,h3,own3,cot_sib=front(ns,x,cot,first_gain[None],decay3,weight3,attention_in)
    vis=jnp.where((context_mask[0]==1)&(q>0),0.0,NEG).astype(F32)
    probs,attended,residual,low2=attention(packed,pairs,segment_ids,vis,x,attention_out,second_gain[None])
    A,B,oo,orr,do,dr=ffn(n,low2,cot,cot_sib,expand_weight,reduce_weight)
    out,rgrad,branch,g2,agrad=call(middle_kernel,[do,dr,residual,second_gain[None],cot,attended,attention_out,oo,orr],[S(BLK,d),S(BLK,d,t=F32),S(BLK,d),S(8,d,t=F32),S(BLK,d)],name="middle")
    dq,dk,dv,dck,dcv=attention_back(packed,pairs,probs,attended,agrad)
    nz,ny=n["z"],n["y"]
    Cf,G,dn=call(grads_kernel,[low,ctx,dq,dk,dv,dck,dcv,attended,branch,attention_in],[S(nz,ny,2,d//ns,4*d),S(CTX,d),S(BLK,d,t=F32)],
       [pltpu.VMEM((d,BLK),BF),pltpu.VMEM((d,CTX),BF),pltpu.VMEM((d,BLK),BF)],name="grads")
    sig,kwg,kdg=conv_back(ns,G,tail_low,low,decay3,weight3,h3)
    igrad,g1=call(last_kernel,[x,first_gain[None],dn,sig,rgrad],[S(BLK,d,t=F32),S(8,d,t=F32)],name="last")
    OA,OB,OC=reduce_all(n,A,B,Cf)
    small=jnp.concatenate([kwg.reshape(nst,d),kdg.reshape(nst,d),jnp.sum(g1,0,keepdims=True),jnp.sum(g2,0,keepdims=True)],0)
    small=lax.psum(small,("grp","seq"))
    rows=d//ns
    mine=lax.dynamic_slice_in_dim(small,q*rows,rows,1)
    rd=d//ns; own=ff//2; rf=own//(nz*ny)
    keep=lax.dynamic_slice_in_dim(OB,c*rd,rd,0); send=lax.dynamic_slice_in_dim(OB,(1-c)*rd,rd,0)
    other=lax.ppermute(send,"seq",[(i,i^1) for i in range(ns)])
    keep=keep.reshape(rd,nz*ny,rf); other=other.reshape(rd,nz*ny,rf)
    eg=jnp.stack([jnp.where(c==0,keep,other),jnp.where(c==0,other,keep)],2).reshape(rd,ff).astype(F32)
    OC=OC.astype(F32)
    return (out[None],igrad[None],mine[2*nst],OC[:,:3*d],mine[:nst].T,mine[nst:2*nst].T,OC[:,3*d:],mine[2*nst+1],eg,OA.astype(F32))

def solution(mesh):
    ins=(P("grp","seq",None),P("grp","seq"),P("grp","seq",None))+(P(),)*8+(P("grp","seq",None),)
    outs=(P("grp","seq",None),)*2+(P("seq"),)+(P("seq",None),)*4+(P("seq"),)+(P("seq",None),)*2
    return jax.shard_map(local,mesh=mesh,in_specs=ins,out_specs=outs,check_vma=False)
```

time: 886 us -> 362 us (0.41)
  matrix products: 351 us -> 0 us
  waiting for transfers between devices: 346 us -> 1.33 us
  Pallas kernels: 0 us -> 318 us
  other arithmetic: 48.5 us -> 4.44 us
  blocking collectives: 41.3 us -> 0 us
  starting transfers between devices: 33.6 us -> 0.11 us
  local copies, waits for them, and re-layouts: 41.8 us -> 21.7 us
    dot_general x63 -> x0, matrix products: 351 us -> none  [the longest x24 113 us: close_right(): jnp.einsum('ckn,nm->ckm', stacked, table, precision=triple, preferred_ele...]
    reduce_scatter x4 -> x0, waiting for transfers between devices: 344 us -> none  [the longest x1 180 us: local(): lax.psum_scatter(reduce_grad, 'seq', scatter_dimension=0, tiled=True)]
    pallas_call x0 -> x9, Pallas kernels: none -> 318 us  [the longest x5 203 us: call(): pl.pallas_call(kernel, out_shape=outs, in_specs=[V] * len(ins), out_specs...]
    unnamed x1 -> x0, blocking collectives: 32 us -> none
    all_to_all x4 -> x0, starting transfers between devices: 29.4 us -> none  [the longest x1 9.82 us: local(): lax.all_to_all(tail_grads.T, 'seq', split_axis=0, concat_axis=1, tiled=True)]
    convert_element_type x14 -> x2, other arithmetic: 20.3 us -> 2.2 us  [the longest x1 2.13 us: local(): OA.astype(F32)]
    reduce_sum x7 -> x2, other arithmetic: 16.7 us -> 0.78 us  [the longest x1 0.77 us: local(): jnp.sum(g1, 0, keepdims=True)]
    psum x1 -> x0, blocking collectives: 9.24 us -> none  [local(): lax.psum(weight_shard_grad.astype(jnp.bfloat16), 'grp').astype(jnp.float32)]
  transfers between devices with their start and end apart: 11 -> 2, of which waited for: 4 -> 1; matrix products, arithmetic and copies ran while one was open for 35% -> 3% of each run, Pallas kernels for 0% -> 40%
where the time goes in v1:
time: 362 us; the launch traced here: 360 us
  Pallas kernels  318 us (88%)
  local copies, waits for them, and re-layouts  21.7 us (6%)
  between operations  14.3 us (4%)
  other arithmetic  4.44 us (1%)
    pallas_call x5, Pallas kernels, call(): pl.pallas_call(kernel, out_shape=outs, in_specs=[V] * len(ins), out_specs...  203 us
    pallas_call x1, Pallas kernels, ffn(): pl.pallas_call(functools.partial(ffn_kernel, n, ff), out_shape=[S(n['z'],...  60.6 us
    pallas_call x1, Pallas kernels, front(): pl.pallas_call(functools.partial(front_kernel, ns, x.shape[0] * ns), out_...  29.2 us
    pallas_call x1, Pallas kernels, attention(): pl.pallas_call(attention_kernel, grid=(HEADS,), in_specs=[pl.BlockSpec((B...  14.8 us
    unnamed x40, local copies, waits for them, and re-layouts  11.7 us
    pallas_call x1, Pallas kernels, attention_back(): pl.pallas_call(attention_back_kernel, grid=(HEADS,), in_specs=[col(BLK, 0...  10.9 us
  transfers between devices with their start and end apart: 2, of which 1 were waited for; matrix products, arithmetic and copies ran while one was open for 3% of the time, Pallas kernels for 40%

profile of v1, /device:TPU:0, one launch (start us, length us, event | category | flops | bytes accessed | tf_op | source)
XLA Modules:
  0.0 360.0 jit_solution(3778514803027068515)
XLA Ops:
  7.2 0.0 all-reduce.2.cloned.1.call-start
  7.2 1.5 copy.23
  8.7 1.5 copy.24
  10.2 0.7 fusion.vis
  10.8 29.2 %front.1 = (bf16[512,1024]{1,0:T(8,128)(2,1)}, bf16[128,1024]{1,0:T(8,128)(2,1)}, bf16[512,3072]{1,0:T(8,128)(2,1)}, bf16[128,1024]{1,0:T(8,128)(2,1)}, bf16[128...) custom-call(bf16[512,1024]{1,0:T(8,128)(2,1)} %bitcast.38, ...), custom_call_target="tpu_custom_call" | custom-call | tf_op jit(solution)/shard_map/front/pallas_call | solution.py:291
  40.0 0.0 copy-done.2
  40.1 1.0 copy-done.3
  41.1 14.8 %attention.1 = (bf16[8,512,640]{2,1,0:T(8,128)(2,1)}, bf16[512,1024]{1,0:T(8,128)(2,1)S(1)}, f32[512,1024]{1,0:T(8,128)S(1)}, bf16[512,1024]{1,0:T(8,128)(2,1)S(1)}) custom-call(bf16[512,3072]{1,0:T(8,128)(2,1)} %get-tuple-element.48.q.k.v, bf16[512,3072]{1,0:T(8,128)(2,1)} %get-tuple-element.48.q.k.v, bf16[512,3072]{1,0:T(8,128)(2,1)} %get-tuple-element.48.q.k.v, ...), custom_call_target="tpu_custom_call" | custom-call | flops 4000000000 | bytes 20000000 | tf_op jit(solution)/shard_map/attention/pallas_call | solution.py:355
  55.9 1.0 copy-done
  56.9 1.3 copy-done.5
  58.2 1.0 copy-done.13
  59.2 60.6 %ffn.1 = (bf16[4,2,256,1024]{3,2,1,0:T(8,128)(2,1)}, bf16[4,2,128,2048]{3,2,1,0:T(8,128)(2,1)}, f32[512,1024]{1,0:T(8,128)}, bf16[512,1024]{1,0:T(8,128)(2,1)}, ...) custom-call(bf16[512,1024]{1,0:T(8,128)(2,1)} %copy-done.13, bf16[512,1024]{1,0:T(8,128)(2,1)} %bitcast.44, ...), custom_call_target="tpu_custom_call" | custom-call | flops 25999998976 | bytes 30000000 | tf_op jit(solution)/shard_map/ffn/pallas_call | solution.py:459
  119.8 0.0 copy-start.1
  119.8 10.6 %middle.1 = (bf16[512,1024]{1,0:T(8,128)(2,1)}, f32[512,1024]{1,0:T(8,128)}, bf16[512,1024]{1,0:T(8,128)(2,1)}, f32[8,1024]{1,0:T(8,128)}, bf16[512,1024]{1,0:T(8,128)(2,1)}) custom-call(f32[512,1024]{1,0:T(8,128)} %get-tuple-element.52.dx_own, bf16[512,1024]{1,0:T(8,128)(2,1)} %get-tuple-element.53.dx_rec, f32[512,1024]{1,0:T(8,128)} %copy-done.5, ...), custom_call_target="tpu_custom_call" | custom-call | flops 1000000000 | bytes 20000000 | tf_op jit(solution)/shard_map/middle/pallas_call | solution.py:499
  130.5 10.9 %attention_back.1 = (bf16[512,1024]{1,0:T(8,128)(2,1)S(1)}, bf16[512,1024]{1,0:T(8,128)(2,1)S(1)}, bf16[512,1024]{1,0:T(8,128)(2,1)S(1)}, bf16[128,1024]{1,0:T(8,128)(2,1)S(1)}, bf16[128,1024]{1,0:T(8,128)(2,1)S(1)}) custom-call(bf16[512,3072]{1,0:T(8,128)(2,1)} %get-tuple-element.48.q.k.v, bf16[512,3072]{1,0:T(8,128)(2,1)} %get-tuple-element.48.q.k.v, ...), custom_call_target="tpu_custom_call" | custom-call | flops 4000000000 | bytes 20000000 | tf_op jit(solution)/shard_map/attention_back/pallas_call | solution.py:524
  141.4 0.0 copy-start.6
  141.4 1.0 copy-done.6
  142.3 1.0 copy-done.7
  143.3 1.0 copy-done.8
  144.3 0.7 copy-done.9
  145.0 0.7 copy-done.10
  145.7 19.4 %grads.1 = (bf16[4,2,2,64,4096]{4,3,2,1,0:T(8,128)(2,1)}, bf16[128,1024]{1,0:T(8,128)(2,1)}, f32[512,1024]{1,0:T(8,128)}) custom-call(bf16[512,1024]{1,0:T(8,128)(2,1)} %get-tuple-element.59.low, bf16[128,1024]{1,0:T(8,128)(2,1)} %get-tuple-element.60.ctx, bf16[512,1024]{1,0:T(8,128)(2,1)} %copy-done.6, bf16[512,1024]{1,0:T(8,128)(2,1)} %copy-done.7, ...), custom_call_target="tpu_custom_call" | custom-call | flops 1000000000 | bytes 20000000 | tf_op jit(solution)/shard_map/grads/pallas_call | solution.py:499
  165.1 20.7 %conv_back.1 = (bf16[512,1024]{1,0:T(8,128)(2,1)}, f32[16,8,128]{2,1,0:T(8,128)}, f32[16,8,128]{2,1,0:T(8,128)}) custom-call(bf16[128,1024]{1,0:T(8,128)(2,1)} %get-tuple-element.70.G, bf16[128,1024]{1,0:T(8,128)(2,1)} %get-tuple-element.71.tail_low, bf16[512,1024]{1,0:T(8,128)(2,1)} %get-tuple-element.59.low, f32[16,8,128]{2,1,0:T(8,128)} %bitcast.51, ...), custom_call_target="tpu_custom_call" | custom-call | flops 1000000000 | bytes 20000000 | tf_op jit(solution)/shard_map/conv_back/pallas_call | solution.py:499
  185.8 0.0 copy-start.17
  185.9 0.0 copy-start.15
  185.9 0.0 copy-start.16
  185.9 6.8 %last.1 = (f32[512,1024]{1,0:T(8,128)}, f32[8,1024]{1,0:T(8,128)}) custom-call(bf16[512,1024]{1,0:T(8,128)(2,1)} %bitcast.39, f32[1,1024]{1,0:T(1,128)} %bitcast.61, f32[512,1024]{1,0:T(8,128)} %get-tuple-element.69.dn, bf16[512,1024]{1,0:T(8,128)(2,1)} %get-tuple-element.73.sig, f32[512,1024]{1,0:T(8,128)} %get-tuple-element.74.rgrad), custom_call_target="tpu_custom_call" | custom-call | flops 1000000000 | bytes 20000000 | tf_op jit(solution)/shard_map/last/pallas_call | solution.py:499
  192.7 0.8 reduce_sum.18
  193.5 0.0 copy-done.17
  193.6 0.7 pad_maximum_fusion
  194.2 0.0 all-reduce.2.cloned.1.call-update
  194.3 145.0 %reduce_all.1 = (bf16[256,1024]{1,0:T(8,128)(2,1)}, bf16[128,2048]{1,0:T(8,128)(2,1)}, bf16[64,4096]{1,0:T(8,128)(2,1)}) custom-call(bf16[4,2,256,1024]{3,2,1,0:T(8,128)(2,1)} %get-tuple-element.80.A, bf16[4,2,128,2048]{3,2,1,0:T(8,128)(2,1)} %get-tuple-element.81.B, bf16[4,2,2,64,4096]{4,3,2,1,0:T(8,128)(2,1)} %get-tuple-element.82.Cf), custom_call_target="tpu_custom_call" | custom-call | flops 1000000000 | bytes 20000000 | tf_op jit(solution)/shard_map/reduce_all/pallas_call | solution.py:499
  339.3 0.0 copy-start.14
  339.3 1.0 constant_dynamic-slice_fusion
  340.4 0.1 collective-permute-start
  340.5 1.9 slice.24
  342.4 1.6 slice.25
  344.0 2.1 convert_element_type.15
  346.1 1.3 all-reduce.2.cloned.1.call-done
  347.5 1.3 dynamic-slice_bitcast_fusion.2
  348.8 1.4 dynamic-slice_bitcast_fusion
  350.2 0.0 collective-permute-done
  350.2 0.1 broadcast_select_fusion.1
  350.3 0.1 copy.27
  350.4 0.1 copy.28
  350.4 0.1 maximum_convert_fusion
  350.5 0.8 copy.22
  351.3 1.8 reshape.106
  (21 shorter events, 0.1 us)
Async XLA Ops:
  7.2 340.3 %all-reduce.2.cloned.1.call-start = ((), (), s32[]{:S(2)}) async-start(), calls=%async_computation | async-start | bytes 327680 | tf_op jit(solution)/shard_map/psum | solution.py:753
  10.8 29.2 %copy-start.2 = (bf16[1,512,1024]{2,1,0:T(8,128)(2,1)S(1)}, bf16[1,512,1024]{2,1,0:T(8,128)(2,1)}, u32[]{:S(2)}) copy-start(bf16[1,512,1024]{2,1,0:T(8,128)(2,1)} %param.12) | copy-start | bytes 3145732
  10.8 29.2 %copy-start.11 = (f32[1024]{0:T(1024)S(1)}, f32[1024]{0:T(1024)}, u32[]{:S(2)}) copy-start(f32[1024]{0:T(1024)} %param.20) | copy-start | bytes 12292
  10.8 29.2 %copy-start.12 = (s32[1,512]{1,0:T(1,128)S(1)}, s32[1,512]{1,0:T(1,128)}, u32[]{:S(2)}) copy-start(s32[1,512]{1,0:T(1,128)} %seg.1) | copy-start | bytes 6148
  40.1 1.0 copy-start.3
  55.9 1.0 copy-start
  56.9 1.3 copy-start.5
  58.2 1.0 copy-start.13
  119.8 10.7 %copy-start.1 = (bf16[512,1024]{1,0:T(8,128)(2,1)S(1)}, bf16[512,1024]{1,0:T(8,128)(2,1)}, u32[]{:S(2)}) copy-start(bf16[512,1024]{1,0:T(8,128)(2,1)} %copy-done) | copy-start | bytes 3145732
  119.8 10.6 %copy-start.4 = (bf16[128,2048]{1,0:T(8,128)(2,1)S(1)}, bf16[128,2048]{1,0:T(8,128)(2,1)}, u32[]{:S(2)}) copy-start(bf16[128,2048]{1,0:T(8,128)(2,1)} %get-tuple-element.49.ck.cv) | copy-start | bytes 1572868
  141.4 1.0 copy-start.6
  142.3 1.0 copy-start.7
  143.3 1.0 copy-start.8
  144.3 0.7 copy-start.9
  145.0 0.7 copy-start.10
  185.8 7.6 %copy-start.17 = (f32[8,1024]{1,0:T(8,128)S(1)}, f32[8,1024]{1,0:T(8,128)}, u32[]{:S(2)}) copy-start(f32[8,1024]{1,0:T(8,128)} %get-tuple-element.79) | copy-start | bytes 98308
  185.9 7.6 %copy-start.15 = (f32[16,8,128]{2,1,0:T(8,128)S(1)}, f32[16,8,128]{2,1,0:T(8,128)}, u32[]{:S(2)}) copy-start(f32[16,8,128]{2,1,0:T(8,128)} %get-tuple-element.76) | copy-start | bytes 196612
  185.9 7.6 %copy-start.16 = (f32[16,8,128]{2,1,0:T(8,128)S(1)}, f32[16,8,128]{2,1,0:T(8,128)}, u32[]{:S(2)}) copy-start(f32[16,8,128]{2,1,0:T(8,128)} %get-tuple-element.77) | copy-start | bytes 196612
  339.3 10.9 %copy-start.14 = (bf16[128,2048]{1,0:T(8,128)(2,1)S(1)}, bf16[128,2048]{1,0:T(8,128)(2,1)}, u32[]{:S(2)}) copy-start(bf16[128,2048]{1,0:T(8,128)(2,1)} %get-tuple-element.84) | copy-start | bytes 1572868
  340.4 9.8 %collective-permute-start = (bf16[64,2048]{1,0:T(8,128)(2,1)S(1)}, bf16[64,2048]{1,0:T(8,128)(2,1)S(1)}, u32[]{:S(2)}, u32[]{:S(2)}) collective-permute-start(bf16[64,2048]{1,0:T(8,128)(2,1)S(1)} %constant_dynamic-slice_fusion), channel_id=1, source_target_pairs={{0,1},{1,0},{2,3},{3,2},{4,5},{5,4},{6,7},{7,6},{8,9},{9,8},{10,11... | collective-permute-start | bytes 786440 | tf_op jit(solution)/shard_map/ppermute | solution.py:758
Sparse Core Ops, SparseCore 0:
  194.4 153.0 all-reduce.1

commit v2 on v1

v2 whole, which is shorter than its diff:
```python
import functools
import heapq
import itertools
import math

import jax
import jax.numpy as jnp
from jax import lax
from jax.experimental import pallas as pl
from jax.experimental.pallas import tpu as pltpu
from jax.sharding import PartitionSpec as P

MESH=pl.DeviceIdType.MESH
BF=jnp.bfloat16

def sizes(nx, ns):
    ny = nx if ns % (2*nx)==0 else 1
    return {"x":nx,"y":ny,"z":ns//(2*ny)}

class Place:
    def __init__(s, n):
        s.n=n; q=lax.axis_index("seq")
        s.i=dict(x=lax.axis_index("grp"), y=lax.rem(lax.div(q,2),n["y"]), z=lax.div(q,2*n["y"])); s.c=lax.rem(q,2)
    def at(s, ax, k):
        return lax.rem(s.i[ax]+k, s.n[ax])
    def device(s, ax, k):
        j=dict(s.i); j[ax]=s.at(ax,k)
        return {"grp":j["x"],"seq":(j["z"]*s.n["y"]+j["y"])*2+s.c}
    def sibling(s):
        return {"seq":(s.i["z"]*s.n["y"]+s.i["y"])*2+1-s.c}
    def partners(s):
        return [s.device(ax,k) for ax in "xyz" for k in range(1,s.n[ax])]

def stage_shapes(n, order, rows, cw):
    left=dict(n); out=[]
    for ax in order:
        del left[ax]
        out.append(tuple(left[a] for a in "zy" if a in left)+(rows, cw*(left["x"] if "x" in left else 1)))
    return out


EPS=1e-5
BLK=512; CTX=128; HEADS=8; HD=128
F32=jnp.float32

def norm_rows(src, gain, dst, rows, step=64):
    def body(i,_):
        rr=pl.ds(pl.multiple_of(i*step,16),step)
        x=src[rr,:].astype(F32)
        x=x-jnp.mean(x,axis=-1,keepdims=True)
        v=jnp.mean(x*x,axis=-1,keepdims=True)
        dst[rr,:]=(x*lax.rsqrt(v+EPS)*gain).astype(BF)
        return 0
    lax.fori_loop(0,rows//step,body,0)

def rates(decay, length):
    return jnp.exp(decay)*(1.0/length)

def block_state(low, rate3, row0, rows, put):
    nst=rate3.shape[0]
    back=7.0-lax.broadcasted_iota(jnp.int32,(8,128),0).astype(F32)
    for lt in range(low.shape[1]//128):
        lanes=pl.ds(lt*128,128)
        r=[jnp.broadcast_to(rate3[n,lt:lt+1,:],(8,128)) for n in range(nst)]
        a8=[jnp.exp(-8.0*v) for v in r]
        def body(g,acc):
            u=low[pl.ds(pl.multiple_of(row0+g*16,16),16),lanes].astype(F32)
            lo,hi=u[:8],u[8:]
            acc=tuple(a*c+lo for a,c in zip(a8,acc))
            return tuple(a*c+hi for a,c in zip(a8,acc))
        acc=lax.fori_loop(0,rows//16,body,tuple(jnp.zeros((8,128),F32) for _ in range(nst)),unroll=2)
        for n in range(nst):
            put(n,lt,jnp.sum(acc[n]*jnp.exp(-back*r[n]),axis=0,keepdims=True))

def split_lanes(src, dst, rows):
    def body(g,_):
        for lt in range(src.shape[1]//128):
            v=src[pl.ds(pl.multiple_of(g*16,16),16),lt*128:(lt+1)*128].astype(F32)
            dst[pl.ds(g*16,16),lt,:]=v
        return 0
    lax.fori_loop(0,rows//16,body,0)

def join_lanes(src, dst, rows):
    def body(g,_):
        for lt in range(dst.shape[1]//128):
            dst[pl.ds(pl.multiple_of(g*16,16),16),lt*128:(lt+1)*128]=src[pl.ds(g*16,16),lt,:].astype(dst.dtype)
        return 0
    lax.fori_loop(0,rows//16,body,0)

class Scan:
    def __init__(s, ns, nst, s3, gather, spread, h3, sem, forward):
        s.ns,s.nst,s.s3,s.gather,s.spread,s.h3=ns,nst,s3,gather,spread,h3
        s.sem=sem; s.forward=forward; s.q=lax.axis_index("seq"); s.stride=ns//nst
        s.n=lax.div(s.q,s.stride); s.scans=lax.rem(s.q,s.stride)==0
    def to_scanner(s, n):
        return pltpu.make_async_remote_copy(src_ref=s.s3.at[n],dst_ref=s.gather.at[s.q],send_sem=s.sem[0].at[n],recv_sem=s.sem[1].at[s.q],device_id={"seq":n*s.stride},device_id_type=MESH)
    def from_block(s, b):
        return pltpu.make_async_remote_copy(src_ref=s.s3.at[0],dst_ref=s.gather.at[b],send_sem=s.sem[0].at[0],recv_sem=s.sem[1].at[b],device_id={"seq":b},device_id_type=MESH)
    def to_block(s, b):
        return pltpu.make_async_remote_copy(src_ref=s.spread.at[b],dst_ref=s.h3.at[s.n],send_sem=s.sem[2].at[b],recv_sem=s.sem[3].at[s.n],device_id={"seq":b},device_id_type=MESH)
    def from_scanner(s, n):
        return pltpu.make_async_remote_copy(src_ref=s.spread.at[0],dst_ref=s.h3.at[n],send_sem=s.sem[2].at[0],recv_sem=s.sem[3].at[n],device_id={"seq":n*s.stride},device_id_type=MESH)
    def each(s, count, fn, skip):
        def body(i,_):
            @pl.when(i!=skip)
            def _(): fn(i)
            return 0
        lax.fori_loop(0,count,body,0)
    def collect(s):
        mine=jnp.where(s.scans,s.n,s.nst)
        s.each(s.nst,lambda n:s.to_scanner(n).start(),mine)
    def scan(s, decay_block):
        mine=jnp.where(s.scans,s.n,s.nst)
        @pl.when(s.scans)
        def _():
            s.gather[s.q]=s.s3[s.n]
            s.each(s.ns,lambda b:s.from_block(b).wait_recv(),s.q)
            a=decay_block[s.n]
            def body(i,h):
                b=i if s.forward else s.ns-1-i
                s.spread[b]=h
                return a*h+s.gather[b]
            lax.fori_loop(0,s.ns,body,jnp.zeros((8,128),F32))
            s.each(s.ns,lambda b:s.to_block(b).start(),s.q)
            s.h3[s.n]=s.spread[s.q]
    def receive(s):
        mine=jnp.where(s.scans,s.n,s.nst)
        s.each(s.nst,lambda n:s.from_scanner(n).wait_recv(),mine)
    def drain(s):
        mine=jnp.where(s.scans,s.n,s.nst)
        s.each(s.nst,lambda n:s.to_scanner(n).wait_send(),mine)
        @pl.when(s.scans)
        def _(): s.each(s.ns,lambda b:s.to_block(b).wait_send(),s.q)

def scan_scratch(ns,nst):
    return [pltpu.VMEM((nst,8,128),F32),pltpu.VMEM((ns,8,128),F32),pltpu.VMEM((ns,8,128),F32),
      pltpu.SemaphoreType.DMA((nst,)),pltpu.SemaphoreType.DMA((ns,)),pltpu.SemaphoreType.DMA((ns,)),pltpu.SemaphoreType.DMA((nst,))]

def front_kernel(ns, length, x, cot, gain, decay3, weight3, w_hbm, low, tail_low, packed, ctx, pairs, h3, own3, cot_sib,
                 w, tail_x, rate3, dec3, u3, y3, s3, gather, spread, e0, e1, e2, e3, wsem, tsem, csem):
    q=lax.axis_index("seq"); c=lax.rem(q,2); g=lax.axis_index("grp")
    nst=decay3.shape[0]
    sem=pltpu.get_barrier_semaphore()
    def sig(i,_):
        @pl.when(i!=q)
        def _(): pl.semaphore_signal(sem,inc=1,device_id={"seq":i},device_id_type=MESH)
        return 0
    lax.fori_loop(0,ns,sig,0)
    wcp=pltpu.make_async_copy(w_hbm,w,wsem); wcp.start()
    pl.semaphore_wait(sem,ns-1)
    tail=pltpu.make_async_remote_copy(src_ref=x.at[pl.ds(BLK-CTX,CTX),:],dst_ref=tail_x,send_sem=tsem.at[0],recv_sem=tsem.at[1],device_id={"seq":jnp.minimum(q+1,ns-1)},device_id_type=MESH)
    @pl.when(q<ns-1)
    def _(): tail.start()
    cc=pltpu.make_async_remote_copy(src_ref=cot,dst_ref=cot_sib,send_sem=csem.at[0],recv_sem=csem.at[1],device_id={"seq":q+1-2*c},device_id_type=MESH)
    cc.start()
    rate3[...]=rates(decay3[...],length)
    dec3[...]=jnp.exp(-float(BLK)*rate3[...])
    norm_rows(x,gain[...],low,BLK)
    def put_own(n,lt,v): own3[n,lt:lt+1,:]=v
    block_state(low,rate3,0,BLK-CTX,put_own)
    @pl.when(q>0)
    def _(): tail.wait_recv()
    @pl.when(q==0)
    def _(): tail_x[...]=jnp.zeros_like(tail_x)
    norm_rows(tail_x,gain[...],tail_low,CTX)
    def put_tail(n,lt,v): s3[n,lt:lt+1,:]=v
    block_state(tail_low,rate3,0,CTX,put_tail)
    for n in range(nst):
        s3[n]=jnp.exp(-float(BLK-CTX)*rate3[n])*s3[n]+own3[n]
    ex=Scan(ns,nst,s3,gather,spread,h3,[e0,e1,e2,e3],True)
    ex.collect()
    wcp.wait()
    def mm(i,_):
        cols=pl.ds(pl.multiple_of(i*256,128),256)
        packed[:,cols]=jnp.dot(low[...],w[:,cols],preferred_element_type=F32).astype(BF)
        return 0
    tiles=packed.shape[1]//256
    lax.fori_loop(0,tiles//2,mm,0)
    ex.scan(dec3)
    split_lanes(tail_low,u3,CTX)
    lax.fori_loop(tiles//2,tiles,mm,0)
    ex.receive()
    a=[jnp.exp(-rate3[n]) for n in range(nst)]
    k=[weight3[n]*jnp.sqrt(rate3[n]) for n in range(nst)]
    def step(t,h):
        u=u3[t]
        h=tuple(p*v+u for p,v in zip(a,h))
        ys=[p*v for p,v in zip(k,h)]
        while len(ys)>1: ys=[ys[i]+ys[i+1] if i+1<len(ys) else ys[i] for i in range(0,len(ys),2)]
        y3[t]=ys[0]
        return h
    lax.fori_loop(0,CTX,step,tuple(h3[n] for n in range(nst)),unroll=2)
    join_lanes(y3,ctx,CTX)
    d=low.shape[1]
    def pm(i,_):
        cols=pl.ds(pl.multiple_of(i*256,128),256)
        pairs[:,cols]=jnp.dot(ctx[...],w[:,pl.ds(pl.multiple_of(d+i*256,128),256)],preferred_element_type=F32).astype(BF)
        return 0
    lax.fori_loop(0,pairs.shape[1]//256,pm,0)
    ex.drain()
    @pl.when(q<ns-1)
    def _(): tail.wait_send()
    cc.wait()

def front(ns, x, cot, gain, decay3, weight3, w):
    nst=decay3.shape[0]; d=x.shape[1]
    V=pl.BlockSpec(memory_space=pltpu.VMEM); A=pl.BlockSpec(memory_space=pl.ANY)
    S=lambda *s,t=BF: jax.ShapeDtypeStruct(s,t)
    return pl.pallas_call(functools.partial(front_kernel,ns,x.shape[0]*ns),
        out_shape=[S(BLK,d),S(CTX,d),S(BLK,3*d),S(CTX,d),S(CTX,2*d),S(nst,8,128,t=F32),S(nst,8,128,t=F32),S(BLK,d)],
        in_specs=[V,A,V,V,V,A],out_specs=[V]*7+[A],
        scratch_shapes=[pltpu.VMEM((d,3*d),BF),pltpu.VMEM((CTX,d),BF),pltpu.VMEM((nst,8,128),F32),pltpu.VMEM((nst,8,128),F32),
          pltpu.VMEM((CTX,8,128),F32),pltpu.VMEM((CTX,8,128),F32)]+scan_scratch(ns,nst)+[pltpu.SemaphoreType.DMA,pltpu.SemaphoreType.DMA((2,)),pltpu.SemaphoreType.DMA((2,))],
        compiler_params=pltpu.CompilerParams(collective_id=0,has_side_effects=True,vmem_limit_bytes=60*2**20),
        name="front")(x,cot,gain,decay3,weight3,w)

NEG=-1e30
NT=(((1,),(1,)),((),()))
TN=(((0,),(0,)),((),()))
NN=(((1,),(0,)),((),()))
def mm(a,b,dims=NN): return lax.dot_general(a,b,dims,preferred_element_type=F32)

def attention_kernel(q,k,v,ck,cv,seg,vis,x,wo,gain,probs,attended,residual,low2,bias):
    h=pl.program_id(0)
    @pl.when(h==0)
    def _():
        row=jnp.broadcast_to(seg[...].astype(F32),(128,BLK))
        col=jnp.transpose(row)
        def body(i,_):
            rr=pl.ds(pl.multiple_of(i*128,128),128)
            qi=i*128+lax.broadcasted_iota(jnp.int32,(128,BLK),0)
            kj=lax.broadcasted_iota(jnp.int32,(128,BLK),1)
            return 0
        for i in range(BLK//128):
            ci=col[i*128:(i+1)*128]
            for j in range(BLK//128):
                if j>i:
                    bias[i*128:(i+1)*128,j*128:(j+1)*128]=jnp.full((128,128),NEG,F32); continue
                ok=ci==row[:,j*128:(j+1)*128]
                if i==j: ok=ok&(lax.broadcasted_iota(jnp.int32,(128,128),0)>=lax.broadcasted_iota(jnp.int32,(128,128),1))
                bias[i*128:(i+1)*128,j*128:(j+1)*128]=jnp.where(ok,0.0,NEG)
        bias[:,BLK:]=jnp.broadcast_to(vis[...],(BLK,CTX))
    scale=1.0/math.sqrt(HD)
    half=BLK//2
    for r in range(2):
        rows=slice(r*half,(r+1)*half); n=(r+1)*half
        s1=mm(q[rows,:],k[:n,:],NT)*scale+bias[rows,:n]
        s2=mm(q[rows,:],ck[...],NT)*scale+bias[rows,BLK:]
        top=jnp.maximum(jnp.max(s1,axis=-1,keepdims=True),jnp.max(s2,axis=-1,keepdims=True))
        e1=jnp.exp(s1-top); e2=jnp.exp(s2-top)
        inv=1.0/(jnp.sum(e1,axis=-1,keepdims=True)+jnp.sum(e2,axis=-1,keepdims=True))
        p1=(e1*inv).astype(BF); p2=(e2*inv).astype(BF)
        probs[0,rows,:n]=p1; probs[0,rows,BLK:]=p2
        if n<BLK: probs[0,rows,n:BLK]=jnp.zeros((half,BLK-n),BF)
        o=mm(p1,v[:n,:])+mm(p2,cv[...])
        attended[rows,pl.ds(pl.multiple_of(h*HD,HD),HD)]=o.astype(BF)
    @pl.when(h==HEADS-1)
    def _():
        def body(i,_):
            rr=pl.ds(pl.multiple_of(i*128,128),128)
            res=x[rr,:].astype(F32)+mm(attended[rr,:],wo[...])
            residual[rr,:]=res
            m=res-jnp.mean(res,axis=-1,keepdims=True)
            var=jnp.mean(m*m,axis=-1,keepdims=True)
            low2[rr,:]=(m*lax.rsqrt(var+EPS)*gain[...]).astype(BF)
            return 0
        lax.fori_loop(0,BLK//128,body,0)

def attention(packed,pairs,seg,vis,x,wo,gain):
    d=x.shape[1]
    S=lambda *s,t=BF: jax.ShapeDtypeStruct(s,t)
    full=lambda a: pl.BlockSpec(a.shape,lambda h:(0,)*a.ndim)
    return pl.pallas_call(attention_kernel,grid=(HEADS,),
      in_specs=[pl.BlockSpec((BLK,HD),lambda h:(0,h)),pl.BlockSpec((BLK,HD),lambda h:(0,HEADS+h)),pl.BlockSpec((BLK,HD),lambda h:(0,2*HEADS+h)),
        pl.BlockSpec((CTX,HD),lambda h:(0,h)),pl.BlockSpec((CTX,HD),lambda h:(0,HEADS+h)),full(seg),full(vis),full(x),full(wo),full(gain)],
      out_specs=[pl.BlockSpec((1,BLK,BLK+CTX),lambda h:(h,0,0)),pl.BlockSpec((BLK,d),lambda h:(0,0)),pl.BlockSpec((BLK,d),lambda h:(0,0)),pl.BlockSpec((BLK,d),lambda h:(0,0))],
      out_shape=[S(HEADS,BLK,BLK+CTX),S(BLK,d),S(BLK,d,t=F32),S(BLK,d)],
      scratch_shapes=[pltpu.VMEM((BLK,BLK+CTX),F32)],
      compiler_params=pltpu.CompilerParams(vmem_limit_bytes=48*2**20),
      cost_estimate=pl.CostEstimate(flops=4*10**9,bytes_accessed=2*10**7,transcendentals=3*10**6),
      name="attention")(packed,packed,packed,pairs,pairs,seg,vis,x,wo,gain)

G0=math.sqrt(2/math.pi); G1=0.044715
def gelu_pair(h):
    h2=h*h
    th=jnp.tanh(h*(G0+G0*G1*h2))
    p=0.5*(1.0+th)
    return h*p, p+h*(0.5*(1.0-th*th))*(G0+3*G0*G1*h2)


def norm_back(v, gain, dy):
    x=v-jnp.mean(v,axis=-1,keepdims=True)
    s=lax.rsqrt(jnp.mean(x*x,axis=-1,keepdims=True)+EPS)
    nrm=x*s
    dn=dy*gain
    dv=(dn-jnp.mean(dn,axis=-1,keepdims=True)-nrm*jnp.mean(dn*nrm,axis=-1,keepdims=True))*s
    return dv, dy*nrm
def fold(v):
    return jnp.sum(v.reshape(v.shape[0]//8,8,v.shape[1]),axis=0)


def S(*s,t=BF): return jax.ShapeDtypeStruct(s,t)


class Lane:
    def __init__(s, place, order, rows, cw, src, out, scratch):
        s.p,s.order,s.rows,s.cw,s.src,s.out=place,order,rows,cw,src,out
        s.recv=scratch[:3]; s.ss,s.rs=scratch[3],scratch[4]
        s.begun=[]
        s.mine=pl.ds(pl.multiple_of(place.i["x"]*cw,128),cw)
    def held(s, stage, fixed):
        if stage==0: return s.src(fixed)
        left=[a for a in "zyx" if a not in s.order[:stage]]
        cols=slice(None)
        if "x" in fixed and "x" in left: cols=pl.ds(pl.multiple_of(fixed["x"]*s.cw,128),s.cw)
        return s.recv[stage-1].at[(0,)+tuple(fixed.get(a,slice(None)) for a in "zy" if a in left)+(slice(None),cols)]
    def copy(s, stage, k):
        ax="x" if stage==3 else s.order[stage]
        if stage==3: src=s.out.at[:,s.mine]; dst=s.out.at[:,s.mine]
        else: src=s.held(stage,{ax:s.p.at(ax,k)}); dst=s.recv[stage].at[k-1]
        return pltpu.make_async_remote_copy(src_ref=src,dst_ref=dst,send_sem=s.ss.at[stage,k-1],recv_sem=s.rs.at[stage,k-1],device_id=s.p.device(ax,k),device_id_type=MESH)
    def start(s, stage):
        for k in range(1,s.p.n["x" if stage==3 else s.order[stage]]):
            s.copy(stage,k).start(); s.begun.append((stage,k))
    def drain(s):
        for stage,k in s.begun: s.copy(stage,k).wait_send()
    def finish(s, stage):
        for st,k in s.begun:
            if st==stage: s.copy(st,k).wait_recv()
        if stage==3: return
        ax=s.order[stage]; n=s.p.n
        left=[a for a in "zy" if a not in s.order[:stage+1]]
        R=s.recv[stage]; step=min(s.rows,32)
        for lead in itertools.product(*[range(n[a]) for a in left]):
            fixed=dict(zip(left,lead)); fixed[ax]=s.p.i[ax]
            own=s.held(stage,fixed)
            def body(r,_):
                rr=pl.ds(pl.multiple_of(r*step,16),step)
                v=own[rr,:].astype(F32)
                for k in range(n[ax]-1): v=v+R[(k,)+lead+(rr,slice(None))].astype(F32)
                if stage==2: s.out[rr,s.mine]=v.astype(BF)
                else: R[(0,)+lead+(rr,slice(None))]=v.astype(BF)
                return 0
            if s.rows==step: body(0,0)
            else: lax.fori_loop(0,s.rows//step,body,0)

def lane_scratch(n, order, rows, cw):
    most=max(n.values())-1
    return [pltpu.VMEM((n[ax]-1,)+sh,BF) for ax,sh in zip(order,stage_shapes(n,order,rows,cw))]+[pltpu.SemaphoreType.DMA((4,most)),pltpu.SemaphoreType.DMA((4,most))]

def cut(ref, place, row0, rows, col0, cw):
    def src(fixed):
        cols=pl.ds(pl.multiple_of(col0+fixed["x"]*cw,128),cw) if "x" in fixed else pl.ds(col0,cw*place.n["x"])
        return ref.at[tuple(fixed.get(a,slice(None)) for a in "zy")+(pl.ds(row0,rows),cols)]
    return src

class Agenda:
    def __init__(s): s.items=[]; s.count=0
    def add(s, when, fn):
        heapq.heappush(s.items,(when,s.count,fn)); s.count+=1
    def run(s, now):
        while s.items and s.items[0][0]<=now: heapq.heappop(s.items)[2]()

def plan_of(n, rf, rb, rc, d, own, orders):
    nx=n["x"]; J=max(1,rf//128); plan=[]; o=iter(orders)
    parts=4 if rf//4>=16 else rf//16
    for i in range(4):
        if i<parts: plan.append(("A",0,i*(rf//parts),rf//parts,0,d//nx,next(o)))
        else: next(o)
    for t in range(4): plan.append(("B",0,0,rb,t*512,512//nx,next(o)))
    for k in range(4): plan.append(("C",k,0,rc,0,d//nx,next(o)))
    plan.append(("S",0,0,rc,0,128,next(o)))
    return plan
ORDERS=["xyz"]*4+["yxz"]*4+["xyz","yxz","xyz","yxz"]+["xyz"]
RELEASE=dict(A=[13.,13.,24.,24.],B=[7.,13.,18.,24.],C=[43.,60.,62.,64.],S=[95.])

def forecast(n, plan):
    free=dict(x=0.,y=0.,z=0.); res={}; seen={}; ev=[]
    for i,p in enumerate(plan):
        j=seen.get(p[0],0); seen[p[0]]=j+1
        heapq.heappush(ev,(RELEASE[p[0]][j],i,0))
    while ev:
        t,i,s=heapq.heappop(ev)
        _,_,r0,r,c0,cw,order=plan[i]
        if s<3:
            ax=order[s]; vol=math.prod(stage_shapes(n,order,r,cw)[s])*4*(n[ax]**2/4 if n[ax]>2 else 1)
        else: ax="x"; vol=r*cw*4
        st=max(t,free[ax]); free[ax]=st+vol/91e3
        res[i,s]=free[ax]+2.0
        if s<3: heapq.heappush(ev,(res[i,s]+0.5,i,s+1))
    return res

def tree(ys):
    ys=list(ys)
    while len(ys)>1: ys=[ys[i]+ys[i+1] if i+1<len(ys) else ys[i] for i in range(0,len(ys),2)]
    return ys[0]

def main_kernel(n, ns, length, plan, packed_w, *refs):
    (low2,cot,cots,w1,w2,residual,gain2,attended,wo,packed,pairs,probs,low,tail_low,ctx,w_in,x,gain1,decay3,weight3,h3,
     out,igrad,OA,OBk,OBr,OC,OS,
     x2,cot2,A,B,Cf,crec,dx_rec,out_rec,OBf,small,small_rec,tailb,tail_in,
     wsem1,wsem2,lsem,xsem,dsem,osem,csem,bsem,tsem,psem,outsem,s3,gather,spread,hb,e0,e1,e2,e3)=refs[:60]
    scr=refs[60:]
    place=Place(n); c=place.c; sib=place.sibling(); q=lax.axis_index("seq"); g=lax.axis_index("grp")
    d=x2.shape[1]; nz,ny=n["z"],n["y"]; nzy=nz*ny; rf=A.shape[2]; rb=B.shape[2]; own=B.shape[3]; rc=crec.shape[3]
    nst=decay3.shape[0]; J=max(1,rf//128); rj=rf//J
    sem=pltpu.get_barrier_semaphore()
    def sg(i,_):
        @pl.when(i!=q)
        def _(): pl.semaphore_signal(sem,inc=1,device_id={"seq":i},device_id_type=MESH)
        return 0
    lax.fori_loop(0,ns,sg,0)
    for k in range(1,n["x"]): pl.semaphore_signal(sem,inc=1,device_id=place.device("x",k),device_id_type=MESH)
    agenda=Agenda(); when=forecast(n,plan)
    outs={"A":OA,"B":OBf,"C":OC,"S":OS}; srcs={"A":lambda k:A,"B":lambda k:B,"C":lambda k:crec.at[k],"S":lambda k:small_rec}
    lanes=[]
    for i,(t,k,r0,r,c0,cw,o) in enumerate(plan):
        oc=(k*d if t=="C" else c0)
        lanes.append(Lane(place,o,r,cw,cut(srcs[t](k),place,r0,r,c0,cw),outs[t].at[pl.ds(r0,r),pl.ds(oc,cw*n["x"])],scr[5*i:5*i+5]))
    index={}
    for i,p in enumerate(plan): index.setdefault(p[0],[]).append(i)
    bcopies=[]
    def bcopy(c0,w):
        h=rb//2; cs=pl.ds(c0,w)
        return pltpu.make_async_remote_copy(src_ref=OBf.at[pl.ds(pl.multiple_of((1-c)*h,16),h),cs],dst_ref=OBr.at[:,cs],send_sem=bsem.at[0,c0//512],recv_sem=bsem.at[1,c0//512],device_id=sib,device_id_type=MESH)
    def chain(i,s):
        def fn():
            lanes[i].finish(s)
            if s<3:
                lanes[i].start(s+1); agenda.add(when[i,s+1],chain(i,s+1))
            elif plan[i][0]=="B":
                c0,w=plan[i][4],plan[i][5]*n["x"]; cs=pl.ds(c0,w); h=rb//2
                bcopy(c0,w).start(); bcopies.append((c0,w))
                OBk[:,cs]=OBf[pl.ds(pl.multiple_of(c*h,16),h),cs]
        return fn
    def launch(i):
        lanes[i].start(0); agenda.add(when[i,0],chain(i,0))

    def forward_part(w1s,w2s,act,dexp):
        tiles=own//512; wd=rj if rj%128==0 else 512; per=512//wd
        def wcopy(b):
            if packed_w: s1=s2=b*wd
            else: s1=s2=lax.rem(b,nzy)*(2*rf)+c*rf+lax.div(b,nzy)*rj
            return (pltpu.make_async_copy(w1.at[:,pl.ds(pl.multiple_of(s1,128),wd)],w1s.at[:,pl.ds(pl.multiple_of(b*wd,128),wd)],wsem1.at[b]),
                    pltpu.make_async_copy(w2.at[pl.ds(pl.multiple_of(s2,16),wd),:],w2s.at[pl.ds(pl.multiple_of(b*wd,16),wd),:],wsem2.at[b]))
        cc=[pltpu.make_async_copy(cot,cot2.at[pl.ds(0,BLK),:],lsem.at[0]),pltpu.make_async_copy(cots,cot2.at[pl.ds(BLK,BLK),:],lsem.at[1]),pltpu.make_async_copy(low2,x2.at[pl.ds(0,BLK),:],lsem.at[2])]
        for v in cc: v.start()
        def go(b,_):
            u,v=wcopy(b); v.start(); u.start(); return 0
        lax.fori_loop(0,own//wd,go,0)
        pl.semaphore_wait(sem,ns-1+n["x"]-1)
        xs=pltpu.make_async_remote_copy(src_ref=low2,dst_ref=x2.at[pl.ds(BLK,BLK),:],send_sem=xsem.at[0],recv_sem=xsem.at[1],device_id=sib,device_id_type=MESH)
        xs.start()
        for v in cc: v.wait()
        for t in range(tiles):
            for b in range(t*per,(t+1)*per): wcopy(b)[1].wait()
            cs=slice(t*512,(t+1)*512)
            u=mm(cot2[...],w2s[cs,:],NT)
            for b in range(t*per,(t+1)*per): wcopy(b)[0].wait()
            if t==0: xs.wait()
            h=mm(x2[...],w1s[:,cs])
            a,gp=gelu_pair(h)
            act[:,cs]=a.astype(BF); dexp[:,cs]=(u*gp).astype(BF)
            v=mm(x2[...],dexp[:,cs],TN).astype(BF)
            for b in range(nzy): B[b//ny,b%ny,:,cs]=v[b*rb:(b+1)*rb]
            launch(index["B"][t])
            agenda.run(7.+5.5*t)
            v=mm(act[:,cs],cot2[...],TN).astype(BF)
            for b in range(512//rj):
                e=t*(512//rj)+b; j,zy=e//nzy,e%nzy
                A[zy//ny,zy%ny,j*rj:(j+1)*rj,:]=v[b*rj:(b+1)*rj]
            ready=((t+1)*512//rj)//nzy*rj
            for i in index["A"]:
                if t*512//rj//nzy*rj<plan[i][2]+plan[i][3]<=ready: launch(i)
            agenda.run(8.5+5.5*t)
        cot2[0:BLK,:]=mm(dexp[BLK:,:],w1s[...],NT).astype(BF)
        dc=pltpu.make_async_remote_copy(src_ref=cot2.at[pl.ds(0,BLK),:],dst_ref=dx_rec,send_sem=dsem.at[0],recv_sem=dsem.at[1],device_id=sib,device_id_type=MESH); dc.start()
        agenda.run(27.)
        cot2[BLK:,:]=mm(act[BLK:,:],w2s[...]).astype(BF)
        oc=pltpu.make_async_remote_copy(src_ref=cot2.at[pl.ds(BLK,BLK),:],dst_ref=out_rec,send_sem=osem.at[0],recv_sem=osem.at[1],device_id=sib,device_id_type=MESH); oc.start()
        agenda.run(29.5)
        x2[0:BLK,:]=mm(dexp[0:BLK,:],w1s[...],NT).astype(BF)
        agenda.run(32.)
        x2[BLK:,:]=mm(act[0:BLK,:],w2s[...]).astype(BF)
        agenda.run(34.5)
        dc.wait(); oc.wait()
    pl.run_scoped(forward_part,pltpu.VMEM((d,own),BF),pltpu.VMEM((own,d),BF),pltpu.VMEM((2*BLK,own),BF),pltpu.VMEM((2*BLK,own),BF))

    def ccopy(k):
        return pltpu.make_async_remote_copy(src_ref=Cf.at[k%2,:,:,1-c],dst_ref=crec.at[k],send_sem=csem.at[0,k],recv_sem=csem.at[1,k],device_id=sib,device_id_type=MESH)
    def send_half(k, part, slot):
        if k>=2: ccopy(k-2).wait_send()
        for r in range(2):
            v=part(slice(r*d//2,(r+1)*d//2)).astype(BF)
            for b in range(nzy):
                e=r*nzy+b
                Cf[slot,e//2//ny,e//2%ny,e%2]=v[b*rc:(b+1)*rc]
        ccopy(k).start()
    def join_half(k, slot):
        ccopy(k).wait_recv()
        def add(z,_):
            for y in range(ny):
                for h in range(rc//16):
                    rr=slice(h*16,h*16+16)
                    crec[k,z,y,rr,:]=(crec[k,z,y,rr,:].astype(F32)+Cf[slot,z,y,c,rr,:].astype(F32)).astype(BF)
            return 0
        lax.fori_loop(0,nz,add,0)
        launch(index["C"][k])

    def rest(res,dq,dk,dv,dck,dcv,lowv,ctxv,ggrad2):
        loads=[pltpu.make_async_copy(residual,res,lsem.at[0]),pltpu.make_async_copy(low,lowv,lsem.at[1]),pltpu.make_async_copy(ctx,ctxv,lsem.at[2])]
        for v in loads: v.start()
        def attention_part(attv,wov,pk,pr,pbuf,branch,agrad):
            more=[pltpu.make_async_copy(attended,attv,lsem.at[3]),pltpu.make_async_copy(wo,wov,lsem.at[4]),pltpu.make_async_copy(packed,pk,lsem.at[5]),pltpu.make_async_copy(pairs,pr,lsem.at[6])]
            for v in more: v.start()
            def pload(h): return pltpu.make_async_copy(probs.at[h],pbuf.at[lax.rem(h,2)],psem.at[lax.rem(h,2)])
            pload(0).start()
            for v in loads: v.wait()
            ggrad2[...]=jnp.zeros_like(ggrad2)
            for part in range(4):
                def body(i,_):
                    rr=pl.ds(pl.multiple_of(part*128+i*64,64),64)
                    dy=x2[rr,:].astype(F32)+dx_rec[rr,:].astype(F32)
                    dvv,gg=norm_back(res[rr,:],gain2[...],dy)
                    stage[rr,:]=(res[rr,:]+x2[pl.ds(pl.multiple_of(BLK+part*128+i*64,64),64),:].astype(F32)+out_rec[rr,:].astype(F32)).astype(BF)
                    r=cot_own[rr,:].astype(F32)+dvv
                    res[rr,:]=r; branch[rr,:]=r.astype(BF)
                    ggrad2[...]+=fold(gg)
                    return 0
                lax.fori_loop(0,2,body,0)
                agenda.run(36.5+1.2*part)
            oc=pltpu.make_async_copy(stage,out,outsem.at[0]); oc.start()
            for v in more: v.wait()
            send_half(0,lambda r: mm(attv[:,r],branch[...],TN),0)
            agenda.add(45.,lambda: join_half(0,0))
            agenda.run(42.)
            agrad[...]=mm(branch[...],wov[...],NT).astype(BF)
            agenda.run(44.)
            scale=1.0/math.sqrt(HD); half=BLK//2
            def head(h,_):
                @pl.when(h<HEADS-1)
                def _(): pload(h+1).start()
                pload(h).wait()
                slot=lax.rem(h,2)
                ql=pl.ds(pl.multiple_of(h*HD,128),HD); kl=pl.ds(pl.multiple_of(d+h*HD,128),HD); vl=pl.ds(pl.multiple_of(2*d+h*HD,128),HD)
                for r in range(2):
                    rows=slice(r*half,(r+1)*half); m=(r+1)*half
                    gr=agrad[rows,ql]
                    dot=jnp.sum(gr.astype(F32)*attv[rows,ql].astype(F32),axis=-1,keepdims=True)
                    p1=pbuf[slot,rows,:m]; p2=pbuf[slot,rows,BLK:]
                    s1=(p1.astype(F32)*(mm(gr,pk[:m,vl],NT)-dot)).astype(BF)
                    s2=(p2.astype(F32)*(mm(gr,pr[:,kl],NT)-dot)).astype(BF)
                    dq[rows,ql]=((mm(s1,pk[:m,kl])+mm(s2,pr[:,ql]))*scale).astype(BF)
                    qr=pk[rows,ql]
                    a1=mm(s1,qr,TN)*scale; a2=mm(s2,qr,TN)*scale; b1=mm(p1,gr,TN); b2=mm(p2,gr,TN)
                    if r==0: first=(a1,a2,b1,b2)
                dk[0:half,ql]=(first[0]+a1[:half]).astype(BF); dk[half:,ql]=a1[half:].astype(BF)
                dv[0:half,ql]=(first[2]+b1[:half]).astype(BF); dv[half:,ql]=b1[half:].astype(BF)
                dck[:,ql]=(first[1]+a2).astype(BF); dcv[:,ql]=(first[3]+b2).astype(BF)
                return 0
            for part in range(4):
                lax.fori_loop(2*part,2*part+2,head,0)
                agenda.run(46.5+2.5*part)
            oc.wait()
        def bigger(cot_,stage_):
            nonlocal cot_own,stage
            cot_own=cot_; stage=stage_
            cl=pltpu.make_async_copy(cot,cot_,lsem.at[7]); cl.start(); cl.wait()
            pl.run_scoped(attention_part,pltpu.VMEM((BLK,d),BF),pltpu.VMEM((d,d),BF),pltpu.VMEM((BLK,3*d),BF),pltpu.VMEM((CTX,2*d),BF),pltpu.VMEM((2,BLK,BLK+CTX),BF),pltpu.VMEM((BLK,d),BF),pltpu.VMEM((BLK,d),BF))
        cot_own=stage=None
        pl.run_scoped(bigger,pltpu.VMEM((BLK,d),BF),pltpu.VMEM((BLK,d),BF))
        def conv_part(w,dn,sig,u3,g3,y3,G,rate3,dec3,sp3,d0,d1,xv,tl,ggrad1,sm):
            loads=[pltpu.make_async_copy(w_in,w,lsem.at[0]),pltpu.make_async_copy(x,xv,lsem.at[1]),pltpu.make_async_copy(tail_low,tl,lsem.at[2])]
            for v in loads: v.start()
            def g1(): send_half(1,lambda r: mm(lowv[:,r],dq[...],TN),1); agenda.add(60.,lambda: join_half(1,1))
            def g2(): send_half(2,lambda r: mm(lowv[:,r],dk[...],TN)+mm(ctxv[:,r],dck[...],TN),0); agenda.add(62.,lambda: join_half(2,0))
            def g3_(): send_half(3,lambda r: mm(lowv[:,r],dv[...],TN)+mm(ctxv[:,r],dcv[...],TN),1); agenda.add(64.,lambda: join_half(3,1))
            g1(); agenda.run(58.); g2(); agenda.run(60.); g3_(); agenda.run(62.)
            for v in loads: v.wait()
            G[...]=(mm(dck[...],w[:,d:2*d],NT)+mm(dcv[...],w[:,2*d:],NT)).astype(BF)
            rate3[...]=rates(decay3[...],length)
            dec3[...]=jnp.exp(-float(BLK)*rate3[...])
            split_lanes(G,g3,CTX)
            a=lambda k: jnp.exp(-rate3[k]); kk=lambda k: weight3[k]*jnp.sqrt(rate3[k])
            av=[a(k) for k in range(nst)]; kv=[kk(k) for k in range(nst)]
            def back(i,gs):
                t=CTX-1-i; v=g3[t]
                gs=tuple(p*z+v for p,z in zip(av,gs))
                y3[t]=tree(p*z for p,z in zip(kv,gs))
                return gs
            gs=lax.fori_loop(0,CTX,back,tuple(jnp.zeros((8,128),F32) for _ in range(nst)),unroll=2)
            for k in range(nst): s3[k]=gs[k]
            ex=Scan(ns,nst,s3,gather,spread,hb,[e0,e1,e2,e3],False)
            ex.collect()
            agenda.run(66.)
            split_lanes(tl,u3,CTX)
            up=lax.broadcasted_iota(jnp.int32,(8,128),0).astype(F32)
            for lt in range(d//128):
                ls=slice(lt*128,(lt+1)*128)
                for part in range(0,nst,8):
                    r=[jnp.broadcast_to(rate3[k,lt:lt+1,:],(8,128)) for k in range(part,part+8)]
                    a8=[jnp.exp(-8.0*v) for v in r]
                    def body(i,cr):
                        acc,der=cr
                        u=lowv[pl.ds(pl.multiple_of(i*16,16),16),ls].astype(F32)
                        for w_ in (u[:8],u[8:]):
                            der=tuple(p*(z+y) for p,z,y in zip(a8,der,acc))
                            acc=tuple(p*y+w_ for p,y in zip(a8,acc))
                        return acc,der
                    zz=tuple(jnp.zeros((8,128),F32) for _ in range(8))
                    acc,der=lax.fori_loop(0,(BLK-CTX)//16,body,(zz,zz))
                    for i,k in enumerate(range(part,part+8)):
                        j=7.0-up
                        sp3[k,lt:lt+1,:]=jnp.sum(jnp.exp(-j*r[i])*(8.0*der[i]+j*acc[i]),axis=0,keepdims=True)
                if lt==2: ex.scan(dec3)
                if lt%2==1: agenda.run(67.+lt)
            for part in range(0,nst,4):
                zz=tuple(jnp.zeros((8,128),F32) for _ in range(4))
                aa=[a(k) for k in range(part,part+4)]
                def fwd(t,cr):
                    h,hp,q0,q1=cr
                    u=u3[t]; gg=g3[t]
                    hp=tuple(p*(z+y) for p,z,y in zip(aa,hp,h))
                    h=tuple(p*z+u for p,z in zip(aa,h))
                    return h,hp,tuple(z+gg*y for z,y in zip(q0,h)),tuple(z+gg*y for z,y in zip(q1,hp))
                h,hp,q0,q1=lax.fori_loop(0,CTX,fwd,(tuple(h3[k] for k in range(part,part+4)),zz,zz,zz),unroll=2)
                for i,k in enumerate(range(part,part+4)):
                    d0[k]=q0[i]; d1[k]=q1[i]
                    m=float(BLK-CTX); am=jnp.exp(-m*rate3[k])
                    sp3[k]=aa[i]*(am*hp[i]+m*am*h[i]+sp3[k])
                agenda.run(75.+.7*part)
            ex.receive()
            for lt in range(d//128):
                ls=slice(lt*128,(lt+1)*128)
                r=[jnp.broadcast_to(rate3[k,lt:lt+1,:],(8,128)) for k in range(nst)]
                a8=[jnp.exp(-8.0*z) for z in r]
                v=tuple(jnp.broadcast_to((weight3[k,lt:lt+1,:]*jnp.sqrt(rate3[k,lt:lt+1,:]))*hb[k,lt:lt+1,:],(8,128))*jnp.exp(-(8.0-up)*r[k]) for k in range(nst))
                def two(v):
                    b=tree(v); v=tuple(p*z for p,z in zip(a8,v))
                    t=tree(v); v=tuple(p*z for p,z in zip(a8,v))
                    return jnp.concatenate([t,b],axis=0),v
                def ownrows(i,v):
                    tb,v=two(v)
                    sig[pl.ds(pl.multiple_of(BLK-CTX-16-i*16,16),16),ls]=tb.astype(BF)
                    return v
                v=lax.fori_loop(0,(BLK-CTX)//16,ownrows,v)
                def tailrows(i,v):
                    tb,v=two(v)
                    row=pl.multiple_of(CTX-16-i*16,16)
                    tailb[pl.ds(row,16),ls]=(tb+y3[pl.ds(row,16),lt,:]).astype(BF)
                    return v
                lax.fori_loop(0,CTX//16,tailrows,v)
                agenda.run(80.+.5*lt)
            bc=pltpu.make_async_remote_copy(src_ref=tailb,dst_ref=tail_in,send_sem=tsem.at[0],recv_sem=tsem.at[1],device_id={"seq":jnp.maximum(q-1,0)},device_id_type=MESH)
            @pl.when(q>0)
            def _(): bc.start()
            def dnr(r):
                rr=slice(r*256,(r+1)*256)
                dn[rr,:]=mm(dq[rr,:],w[:,:d],NT)+mm(dk[rr,:],w[:,d:2*d],NT)+mm(dv[rr,:],w[:,2*d:],NT)
            dnr(0); agenda.run(87.); dnr(1); agenda.run(89.)
            ggrad1[...]=jnp.zeros_like(ggrad1)
            def lastrows(i,_):
                rr=pl.ds(pl.multiple_of(i*64,64),64)
                dvv,gg=norm_back(xv[rr,:].astype(F32),gain1[...],dn[rr,:]+sig[rr,:].astype(F32))
                res[rr,:]=res[rr,:]+dvv
                ggrad1[...]+=fold(gg)
                return 0
            lax.fori_loop(0,(BLK-CTX)//64,lastrows,0)
            agenda.run(92.)
            @pl.when(q==ns-1)
            def _(): tail_in[...]=jnp.zeros_like(tail_in)
            @pl.when(q<ns-1)
            def _(): bc.wait_recv()
            sig[BLK-CTX:,:]=tail_in[...]
            lax.fori_loop((BLK-CTX)//64,BLK//64,lastrows,0)
            ic=pltpu.make_async_copy(res,igrad,outsem.at[1]); ic.start()
            sm[...]=jnp.zeros_like(sm)
            for k in range(nst):
                r=rate3[k]; D1=d1[k]+hb[k]*sp3[k]; sq=jnp.sqrt(r)
                kw=sq*d0[k]; kd=weight3[k]*sq*(0.5*d0[k]-r*D1)
                for lt in range(d//128):
                    sm[k:k+1,lt*128:(lt+1)*128]=kw[lt:lt+1,:]; sm[nst+k:nst+k+1,lt*128:(lt+1)*128]=kd[lt:lt+1,:]
            sm[2*nst:2*nst+1,:]=jnp.sum(ggrad1[...],axis=0,keepdims=True)
            sm[2*nst+1:2*nst+2,:]=jnp.sum(ggrad2[...],axis=0,keepdims=True)
            for j in range(d//128):
                v=jnp.transpose(sm[:,j*128:(j+1)*128]).astype(BF)
                for b in range(128//rc):
                    e=j*(128//rc)+b
                    small[e//2//ny,e//2%ny,e%2,:,0:128]=v[b*rc:(b+1)*rc]
                    small[e//2//ny,e//2%ny,e%2,:,128:]=jnp.zeros((rc,small.shape[4]-128),BF)
            sc=pltpu.make_async_remote_copy(src_ref=small.at[:,:,1-c],dst_ref=small_rec,send_sem=csem.at[0,4],recv_sem=csem.at[1,4],device_id=sib,device_id_type=MESH)
            sc.start()
            def join_small():
                sc.wait_recv()
                for z in range(nz):
                    for y in range(ny):
                        small_rec[z,y]=(small_rec[z,y].astype(F32)+small[z,y,c].astype(F32)).astype(BF)
                launch(index["S"][0])
            agenda.add(97.,join_small)
            agenda.run(98.)
            ic.wait(); sc.wait_send(); ex.drain()
            @pl.when(q>0)
            def _(): bc.wait_send()
        M=pltpu.VMEM; st=(nst,8,128)
        pl.run_scoped(conv_part,M((d,3*d),BF),M((BLK,d),F32),M((BLK,d),BF),M((CTX,8,128),F32),M((CTX,8,128),F32),M((CTX,8,128),F32),M((CTX,d),BF),M(st,F32),M(st,F32),M(st,F32),M(st,F32),M(st,F32),M((BLK,d),BF),M((CTX,d),BF),M((8,d),F32),M((128,d),F32))
    M=pltpu.VMEM
    pl.run_scoped(rest,M((BLK,d),F32),M((BLK,d),BF),M((BLK,d),BF),M((BLK,d),BF),M((CTX,d),BF),M((CTX,d),BF),M((BLK,d),BF),M((CTX,d),BF),M((8,d),F32))
    agenda.run(1e9)
    for v in bcopies: bcopy(*v).wait()
    for v in lanes: v.drain()
    for k in (2,3): ccopy(k).wait_send()

def main(n, ns, low2,cot,cots,w1,w2,residual,gain2,attended,wo,packed,pairs,probs,low,tail_low,ctx,w_in,x,gain1,decay3,weight3,h3):
    d=x.shape[1]; ff=w1.shape[1]; nz,ny,nx=n["z"],n["y"],n["x"]; nzy=nz*ny; own=ff//2; rf=own//nzy; rb=d//nzy; rc=d//ns; nst=decay3.shape[0]
    J=max(1,rf//128); rj=rf//J
    packed_w=rj%128!=0
    if packed_w:
        c=lax.rem(lax.axis_index("seq"),2)
        w1=lax.dynamic_index_in_dim(w1.reshape(d,nzy,2,rf),c,2,keepdims=False).reshape(d,own)
        w2=lax.dynamic_index_in_dim(w2.reshape(nzy,2,rf,d),c,1,keepdims=False).reshape(own,d)
    plan=plan_of(n,rf,rb,rc,d,own,ORDERS)
    V=pl.BlockSpec(memory_space=pltpu.VMEM); Y=pl.BlockSpec(memory_space=pl.ANY); M=pltpu.VMEM; D=pltpu.SemaphoreType.DMA
    wd=rj if not packed_w else 512
    scr=[M((2*BLK,d),BF),M((2*BLK,d),BF),M((nz,ny,rf,d),BF),M((nz,ny,rb,own),BF),M((2,nz,ny,2,rc,d),BF),M((4,nz,ny,rc,d),BF),M((BLK,d),BF),M((BLK,d),BF),
         M((rb,own),BF),M((nz,ny,2,rc,128*nx),BF),M((nz,ny,rc,128*nx),BF),M((CTX,d),BF),M((CTX,d),BF),
         D((own//wd,)),D((own//wd,)),D((8,)),D((2,)),D((2,)),D((2,)),D((2,5)),D((2,4)),D((2,)),D((2,)),D((2,))]
    sc=scan_scratch(ns,nst)
    scr+=[sc[0],sc[1],sc[2],M((nst,8,128),F32)]+sc[3:]
    for (t,k,r0,r,c0,cw,o) in plan: scr+=lane_scratch(n,o,r,cw)
    ins=[low2,cot,cots,w1,w2,residual,gain2,attended,wo,packed,pairs,probs,low,tail_low,ctx,w_in,x,gain1,decay3,weight3,h3]
    small_in={6,17,18,19,20}
    return pl.pallas_call(functools.partial(main_kernel,n,ns,BLK*ns,plan,packed_w),
        out_shape=[S(BLK,d),S(BLK,d,t=F32),S(rf,d),S(rc,own),S(rc,own),S(rc,4*d),S(rc,128*nx)],
        in_specs=[V if i in small_in else Y for i in range(len(ins))],out_specs=[Y,Y]+[V]*5,scratch_shapes=scr,
        compiler_params=pltpu.CompilerParams(collective_id=1,has_side_effects=True,vmem_limit_bytes=63*10**6),
        cost_estimate=pl.CostEstimate(flops=45*10**9,bytes_accessed=6*10**7,transcendentals=2*10**6),name="main")(*ins)

def local(layer_input,segment_ids,context_mask,first_gain,attention_in,kernel_weight,kernel_decay,attention_out,second_gain,expand_weight,reduce_weight,cotangent):
    ns=lax.axis_size("seq"); nx=lax.axis_size("grp"); nst=kernel_decay.shape[1]; n=sizes(nx,ns)
    q=lax.axis_index("seq"); c=lax.rem(q,2)
    x=layer_input[0]; cot=cotangent[0]; d=x.shape[1]; ff=expand_weight.shape[1]
    decay3=kernel_decay.T.reshape(nst,8,128); weight3=kernel_weight.T.reshape(nst,8,128)
    low,tail_low,packed,ctx,pairs,h3,own3,cot_sib=front(ns,x,cot,first_gain[None],decay3,weight3,attention_in)
    vis=jnp.where((context_mask[0]==1)&(q>0),0.0,NEG).astype(F32)
    probs,attended,residual,low2=attention(packed,pairs,segment_ids,vis,x,attention_out,second_gain[None])
    out,igrad,OA,keep,other,OC,OS=main(n,ns,low2,cot,cot_sib,expand_weight,reduce_weight,residual,second_gain[None],attended,attention_out,packed,pairs,probs,low,tail_low,ctx,attention_in,x,first_gain[None],decay3,weight3,h3)
    nzy=n["z"]*n["y"]; rd=d//ns; rf=ff//2//nzy; J=max(1,rf//128); rj=rf//J
    keep=keep.reshape(rd,J,nzy,rj); other=other.reshape(rd,J,nzy,rj)
    eg=jnp.stack([jnp.where(c==0,keep,other),jnp.where(c==0,other,keep)],3)
    eg=eg.transpose(0,2,3,1,4).reshape(rd,ff).astype(F32)
    OS=OS.astype(F32)
    return (out[None],igrad[None],OS[:,2*nst],OC[:,d:].astype(F32),OS[:,:nst],OS[:,nst:2*nst],OC[:,:d].astype(F32),OS[:,2*nst+1],eg,OA.astype(F32))

def solution(mesh):
    ins=(P("grp","seq",None),P("grp","seq"),P("grp","seq",None))+(P(),)*8+(P("grp","seq",None),)
    outs=(P("grp","seq",None),)*2+(P("seq"),)+(P("seq",None),)*4+(P("seq"),)+(P("seq",None),)*2
    return jax.shard_map(local,mesh=mesh,in_specs=ins,out_specs=outs,check_vma=False)
```

time: 362 us -> 238 us (0.66)
  Pallas kernels: 318 us -> 207 us
  between operations: 14.3 us -> 0.94 us
  local copies, waits for them, and re-layouts: 21.7 us -> 16.2 us
  other arithmetic: 4.44 us -> 8.24 us
    pallas_call x7 -> x1, Pallas kernels: 274 us -> 164 us  [main(): pl.pallas_call(functools.partial(main_kernel, n, ns, BLK * ns, plan, pack...]
    convert_element_type x1 -> x4, other arithmetic: 0.07 us -> 4.39 us  [the longest x1 1.93 us: local(): OC[:, d:].astype(F32)]
    unnamed x40 -> x24, local copies, waits for them, and re-layouts: 11.7 us -> 12.3 us
  transfers between devices with their start and end apart: 2 -> 0, of which waited for: 1 -> 0; matrix products, arithmetic and copies ran while one was open for 3% -> 0% of each run, Pallas kernels for 40% -> 0%
where the time goes in v2:
time: 238 us; the launch traced here: 233 us
  Pallas kernels  207 us (87%)
  local copies, waits for them, and re-layouts  16.2 us (7%)
  other arithmetic  8.24 us (3%)
    pallas_call x1, Pallas kernels, main(): pl.pallas_call(functools.partial(main_kernel, n, ns, BLK * ns, plan, pack...  164 us
    pallas_call x1, Pallas kernels, front(): pl.pallas_call(functools.partial(front_kernel, ns, x.shape[0] * ns), out_...  29.1 us
    pallas_call x1, Pallas kernels, attention(): pl.pallas_call(attention_kernel, grid=(HEADS,), in_specs=[pl.BlockSpec((B...  14.8 us
    unnamed x24, local copies, waits for them, and re-layouts  12.3 us

profile of v2, /device:TPU:0, one launch (start us, length us, event | category | flops | bytes accessed | tf_op | source)
XLA Modules:
  0.0 232.9 jit_solution(9024364892415790195)
XLA Ops:
  0.6 0.7 fusion.vis
  1.3 1.5 copy.29
  2.8 1.5 copy.28
  4.3 0.0 copy-start
  4.3 0.0 copy-start.2
  4.3 0.0 copy-start.3
  4.3 29.1 %front.1 = (bf16[512,1024]{1,0:T(8,128)(2,1)}, bf16[128,1024]{1,0:T(8,128)(2,1)}, bf16[512,3072]{1,0:T(8,128)(2,1)}, bf16[128,1024]{1,0:T(8,128)(2,1)}, bf16[128...) custom-call(bf16[512,1024]{1,0:T(8,128)(2,1)} %bitcast.26, ...), custom_call_target="tpu_custom_call" | custom-call | tf_op jit(solution)/shard_map/front/pallas_call | solution.py:209
  33.4 0.0 copy-done
  33.4 0.0 copy-done.2
  33.4 0.0 copy-done.3
  33.4 0.0 copy-start.1
  33.4 1.0 copy-done.1
  34.5 14.8 %attention.1 = (bf16[8,512,640]{2,1,0:T(8,128)(2,1)}, bf16[512,1024]{1,0:T(8,128)(2,1)S(1)}, f32[512,1024]{1,0:T(8,128)S(1)}, bf16[512,1024]{1,0:T(8,128)(2,1)S(1)}) custom-call(bf16[512,3072]{1,0:T(8,128)(2,1)} %get-tuple-element.28.q.k.v.refs_9_, bf16[512,3072]{1,0:T(8,128)(2,1)} %get-tuple-element.28.q.k.v.refs_9_, ...), custom_call_target="tpu_custom_call" | custom-call | flops 4000000000 | bytes 20000000 | tf_op jit(solution)/shard_map/attention/pallas_call | solution.py:273
  49.2 0.0 copy-start.4
  49.2 1.3 copy-done.4
  50.5 0.0 copy-start.5
  50.6 1.0 copy-done.5
  51.5 0.0 copy-start.6
  51.5 1.0 copy-done.6
  52.5 163.6 %main.1 = (bf16[512,1024]{1,0:T(8,128)(2,1)}, f32[512,1024]{1,0:T(8,128)}, bf16[256,1024]{1,0:T(8,128)(2,1)}, bf16[64,2048]{1,0:T(8,128)(2,1)}, bf16[64,2048]{1,...) custom-call(bf16[512,1024]{1,0:T(8,128)(2,1)} %copy-done.6, bf16[512,1024]{1,0:T(8,128)(2,1)} %bitcast.36, ...), custom_call_target="tpu_custom_call" | custom-call | flops 44999999488 | bytes 60000000 | tf_op jit(solution)/shard_map/main/pallas_call | solution.py:732
  216.1 0.8 convert_element_type.21
  216.9 0.7 slice_reduce_fusion
  217.6 0.9 fusion.1
  218.4 0.7 copy.27
  219.1 0.7 copy.26
  219.8 1.6 slice_convert_fusion.1
  221.4 1.9 slice_convert_fusion
  223.3 1.1 select_bitcast_fusion.1
  224.5 0.1 convert_bitcast_fusion
  224.6 0.6 copy.25
  225.1 0.0 copy-start.7
  225.2 1.8 reshape.98
  227.0 2.1 convert_element_type.27
  229.1 2.3 copy.34
  231.4 0.0 copy-done.7
  231.4 1.3 copy.35
  (2 shorter events, 0.1 us)
Async XLA Ops:
  4.3 29.1 %copy-start = (bf16[1,512,1024]{2,1,0:T(8,128)(2,1)S(1)}, bf16[1,512,1024]{2,1,0:T(8,128)(2,1)}, u32[]{:S(2)}) copy-start(bf16[1,512,1024]{2,1,0:T(8,128)(2,1)} %param.12) | copy-start | bytes 3145732
  4.3 29.1 %copy-start.2 = (f32[1024]{0:T(1024)S(1)}, f32[1024]{0:T(1024)}, u32[]{:S(2)}) copy-start(f32[1024]{0:T(1024)} %param.20) | copy-start | bytes 12292
  4.3 29.1 %copy-start.3 = (s32[1,512]{1,0:T(1,128)S(1)}, s32[1,512]{1,0:T(1,128)}, u32[]{:S(2)}) copy-start(s32[1,512]{1,0:T(1,128)} %seg.1) | copy-start | bytes 6148
  33.4 1.0 copy-start.1
  49.2 1.3 copy-start.4
  50.5 1.0 copy-start.5
  51.5 1.0 copy-start.6
  225.1 6.2 %copy-start.7 = (f32[512,1024]{1,0:T(8,128)S(1)}, f32[512,1024]{1,0:T(8,128)}, u32[]{:S(2)}) copy-start(f32[512,1024]{1,0:T(8,128)} %get-tuple-element.40) | copy-start | bytes 6291460
